TPU v7x, 32 devices: a whole 2x2x4 slice. The times are simulated.
32 devices in a mesh: row: 8 (over z, x), col: 4 (over y, core).
Axes of the slice: x: 2, y: 2, z: 4, core: 2. Of those that a mesh axis runs over, the one named last changes fastest.
Arguments:
- block_values: bfloat16 [8, 4, 256, 128, 128], P('row', 'col')
- block_rows: int32 [8, 4, 256], P('row', 'col'), may hold values from -1 to 511, as said below
- block_cols: int32 [8, 4, 256], P('row', 'col'), may hold values from -1 to 511, as said below
- cost_vec: float32 [262144], P('col')
- demand: float32 [524288], P('row')
- lower: float32 [262144], P('col'), may hold values from -1.5 to -0.2
- upper: float32 [262144], P('col'), may hold values from 0.2 to 1.5
- bound_kind: int32 [262144], P('col'), may hold values from 0 to 3
- primal_start: float32 [262144], P('col'), may hold values from -4 to 4
- dual_start: float32 [524288], P('row'), may hold values from 0 to 1.5
Outputs:
- primal_out: float32 [262144], P('col')
- dual_out: float32 [524288], P('row')
Inputs may be any that keep to these rules, and one draw needn't show every extreme that they name: A slot's block_rows and block_cols are both -1 exactly when the slot is empty; the live slots of a device come first, a device has at least 128 of them, and in every draw some device has all 256 slots live and some device has empty slots; every block row and every block column of the whole matrix is named by some live slot; a block place may be named by several slots. `block_cols`: as for block_rows.
All inputs are finite; a program needn't handle non-finite values.
Results may differ from a plain program's by a relative error of at most 0.0073.
Values sent between devices are 32-bit elements; how exact they have to be, the bound alone decides.
No kernel may reach another device: no remote copies, remote signals or barrier semaphores. Data moves between devices by JAX's collectives and lax.ppermute only.
A program may use at most 64 MiB of HBM per device.

v0:
```python
import functools

import jax
import jax.numpy as jnp
from jax import lax
from jax.experimental import pallas as pl
from jax.experimental.pallas import tpu as pltpu
from jax.sharding import PartitionSpec as P

SMALL_EPS = 1e-06
STEP_SCALE = 0.3

CHUNKS = 8
GROUP = 32
AHEAD = 3
ROW_HALVING = 1
QUARTERS = 4
FIRST_VMEM = 44 * 1024 * 1024
BLOCK_VMEM = 16 * 1024 * 1024
SMALL_VMEM = 8 * 1024 * 1024


def bit_of(index, bit):
    return jnp.where((index & bit) != 0, 1, 0)


def row_mask():
    return bit_of(lax.axis_index("col"), ROW_HALVING) * (CHUNKS // 2)


def col_mask():
    return (lax.axis_index("row") & (QUARTERS - 1)) * (CHUNKS // QUARTERS)


def col_place(tile, count, mask):
    return jnp.where(tile < 0, count, tile ^ (mask * (count // CHUNKS)))


def row_place(tile, count, mask):
    return jnp.where(tile < 0, count, tile ^ (mask * (count // CHUNKS)))


def chunk_rows(chunk, size):
    return pl.ds(pl.multiple_of(chunk * size, size), size)


def piece_chunk(pieces, place, size):
    per_piece = CHUNKS // len(pieces)
    start = (place % per_piece) * size
    return pieces[place // per_piece], pl.ds(start, size)


def store_pieces(acc, pieces, count):
    size = count // len(pieces)
    for index, piece in enumerate(pieces):
        piece[...] = acc[pl.ds(index * size, size), :]


def add_row(acc, place, term, combine):
    acc[pl.ds(place, 1), :] = combine(acc[pl.ds(place, 1), :], term)


def one_row(ref, tile):
    return ref[pl.ds(jnp.maximum(tile, 0), 1), :]


def tree_sum(parts):
    while len(parts) > 1:
        parts = [parts[i] + parts[i + 1] for i in range(0, len(parts), 2)]
    return parts[0]


def fold_rows(values):
    return jnp.sum(values.reshape(-1, 8, values.shape[-1]), axis=0)


def block_copy(index, values_ref, blocks, arrived):
    part = pl.ds(pl.multiple_of(index * GROUP, GROUP), GROUP)
    return pltpu.make_async_copy(values_ref.at[part], blocks.at[part], arrived.at[index])


def for_slots(ids_ref, visit, finish, before=None):
    count = ids_ref.shape[0] // 2

    def step(index, carry):
        if before is not None:
            before(index)
        slots = [index * GROUP + inner for inner in range(GROUP)]
        ids = [(ids_ref[slot], ids_ref[count + slot]) for slot in slots]
        terms = visit(slots, ids)
        for (row, col), term in zip(ids, terms):
            finish(row, col, term)
        return carry

    lax.fori_loop(0, count // GROUP, step, 0)


def product_terms(vector_ref, tiles, blocks):
    width = vector_ref.shape[1]
    place = lax.broadcasted_iota(jnp.int32, (8, width), 0)
    terms = []
    for start in range(0, len(tiles), 4):
        rows = [one_row(vector_ref, tile) for tile in tiles[start : start + 4]]
        left = jnp.where(place == 0, rows[0], jnp.where(place == 1, rows[1], 0.0))
        right = jnp.where(place == 2, rows[2], jnp.where(place == 3, rows[3], 0.0))
        quad = blocks[start : start + 4]
        found = jnp.dot(
            jnp.concatenate([left, right], axis=1).astype(jnp.bfloat16),
            jnp.concatenate(
                [jnp.concatenate(quad[:2], axis=1), jnp.concatenate(quad[2:], axis=1)], axis=0
            ),
            preferred_element_type=jnp.float32,
        )
        for index in range(4):
            side = (index % 2) * width
            terms.append(found[index : index + 1, side : side + width])
    return terms


def row_max(values):
    return jnp.max(values, axis=0, keepdims=True)


def packed_max(values):
    folded = jnp.max(values.reshape(-1, 16, values.shape[-1]), axis=0)
    return row_max(folded.astype(jnp.float32))


def first_pass_kernel(count, ids_ref, values_ref, *refs):
    row_out, col_out, blocks = refs[:2], refs[2:6], refs[6]
    arrived, row_acc, col_acc = refs[7:]
    mask, across = col_mask(), row_mask()
    groups = values_ref.shape[0] // GROUP
    for index in range(min(AHEAD, groups)):
        block_copy(index, values_ref, blocks, arrived).start()
    for acc in (row_acc, col_acc):
        acc[...] = jnp.zeros_like(acc)

    def before(index):
        block_copy(index, values_ref, blocks, arrived).wait()

        @pl.when(index + AHEAD < groups)
        def _():
            block_copy(index + AHEAD, values_ref, blocks, arrived).start()

    def visit(slots, ids):
        sizes = [jnp.abs(blocks[slot]) for slot in slots]
        return [(packed_max(size.T), packed_max(size)) for size in sizes]

    def finish(row, col, terms):
        add_row(row_acc, row_place(row, count, across), terms[0], jnp.maximum)
        add_row(col_acc, col_place(col, count, mask), terms[1], jnp.maximum)

    for_slots(ids_ref, visit, finish, before)
    store_pieces(row_acc, row_out, count)
    store_pieces(col_acc, col_out, count)


def first_product_kernel(count, ids_ref, blocks, dual_ref, *refs):
    product_out, turned, product_acc = refs[:4], refs[4], refs[5]
    mask = col_mask()
    product_acc[...] = jnp.zeros_like(product_acc)

    def visit(slots, ids):
        found = [blocks[slot] for slot in slots]
        for slot, block in zip(slots, found):
            turned[slot] = block.T
        return product_terms(dual_ref, [row for row, _ in ids], found)

    def finish(row, col, term):
        add_row(product_acc, col_place(col, count, mask), term, jnp.add)

    for_slots(ids_ref, visit, finish)
    store_pieces(product_acc, product_out, count)


def second_pass_kernel(count, ids_ref, blocks, *refs):
    row_in, col_in, row_out, col_out = refs[:2], refs[2:6], refs[6:8], refs[8:12]
    row_scale, col_scale, row_acc, col_acc = refs[12:]
    mask, across = col_mask(), row_mask()
    size = count // CHUNKS
    row_acc[...] = jnp.zeros_like(row_acc)
    col_acc[...] = jnp.zeros_like(col_acc)
    for place in range(CHUNKS):
        piece, part = piece_chunk(row_in, place, size)
        row_scale[chunk_rows(place ^ across, size), :] = lax.rsqrt(piece[part, :] + SMALL_EPS)
        piece, part = piece_chunk(col_in, place, size)
        col_scale[chunk_rows(place ^ mask, size), :] = lax.rsqrt(piece[part, :] + SMALL_EPS)
    width = blocks.shape[-1]
    square = (width, width)
    diagonal = lax.broadcasted_iota(jnp.int32, square, 0) == lax.broadcasted_iota(
        jnp.int32, square, 1
    )
    diagonal = diagonal.astype(jnp.float32).astype(jnp.bfloat16)

    def peaks(row, col, slot):
        sizes = jnp.abs(blocks[slot])
        by_col = sizes.astype(jnp.float32) * one_row(col_scale, col)
        scale = one_row(row_scale, row)
        high = scale.astype(jnp.bfloat16)
        low = (scale - high.astype(jnp.float32)).astype(jnp.bfloat16)
        by_row = jnp.dot(
            jnp.concatenate([diagonal * high, diagonal * low], axis=1),
            jnp.concatenate([sizes, sizes], axis=0),
            preferred_element_type=jnp.float32,
        )
        return row_max(by_col.T), row_max(by_row)

    def visit(slots, ids):
        return [peaks(row, col, slot) for slot, (row, col) in zip(slots, ids)]

    def finish(row, col, terms):
        add_row(row_acc, row_place(row, count, across), terms[0], jnp.maximum)
        add_row(col_acc, col_place(col, count, mask), terms[1], jnp.maximum)

    for_slots(ids_ref, visit, finish)
    for place in range(CHUNKS):
        part = pl.ds(place * size, size)
        piece, inside = piece_chunk(row_out, place, size)
        piece[inside, :] = row_acc[part, :] * row_scale[chunk_rows(place ^ across, size), :]
        piece, inside = piece_chunk(col_out, place, size)
        piece[inside, :] = col_acc[part, :] * col_scale[chunk_rows(place ^ mask, size), :]


def row_scale_kernel(count, near, far, scale_ref, vector_ref, new_scale, squares):
    across = row_mask()
    size = count // CHUNKS
    sums = []
    for place in range(CHUNKS):
        part = chunk_rows(place ^ across, size)
        piece, inside = piece_chunk((near, far), place, size)
        scale = scale_ref[part, :] * lax.rsqrt(piece[inside, :] + SMALL_EPS)
        new_scale[part, :] = scale
        scaled = scale * vector_ref[part, :]
        sums.append(fold_rows(scaled * scaled))
    half = CHUNKS // 2
    squares[...] = tree_sum(sums[:half]) + tree_sum(sums[half:])


def col_scale_kernel(count, *refs):
    pieces, (scale_ref, vector_ref, new_scale, squares, demand_squares) = refs[:4], refs[4:]
    mask = col_mask()
    size = count // CHUNKS
    sums = []
    for place in range(CHUNKS):
        part = chunk_rows(place ^ mask, size)
        piece, inside = piece_chunk(pieces, place, size)
        scale = scale_ref[part, :] * lax.rsqrt(piece[inside, :] + SMALL_EPS)
        new_scale[part, :] = scale
        scaled = scale * vector_ref[part, :]
        sums.append(fold_rows(scaled * scaled))
    squares[...] = tree_sum(sums)
    tail = pl.ds(pieces[0].shape[0] - 8, 8)
    demand_squares[...] = tree_sum([piece[tail, :] for piece in pieces])


def norm_ratio(cost_squares, demand_squares):
    cost_total = jnp.sum(cost_squares[...], keepdims=True)
    demand_total = jnp.sum(demand_squares[...], keepdims=True)
    return jnp.sqrt(cost_total + SMALL_EPS) / jnp.sqrt(demand_total + SMALL_EPS)


def forward_kernel(count, first, last, ids_ref, turned, *refs):
    product, refs = refs[:4], refs[4:]
    scale_ref, cost_ref, low_ref, high_ref, kind_ref, primal_ref = refs[:6]
    cost_squares, demand_squares, primal_out = refs[6:9]
    row_out, (shifted, row_acc) = refs[9:11], refs[11:]
    mask, across = col_mask(), row_mask()
    size = count // CHUNKS
    row_acc[...] = jnp.zeros_like(row_acc)
    primal_step = STEP_SCALE / norm_ratio(cost_squares, demand_squares)
    for place in range(CHUNKS):
        part = chunk_rows(place ^ mask, size)
        piece, inside = piece_chunk(product, place, size)
        scale = scale_ref[part, :]
        inverse = 1.0 / scale
        primal = primal_ref[part, :]
        if first:
            primal = primal * inverse
        gradient = scale * piece[inside, :]
        moved = primal - primal_step * (scale * cost_ref[part, :] - gradient)
        kind = kind_ref[part, :]
        moved = jnp.where(
            (kind == 1) | (kind == 3), jnp.maximum(moved, low_ref[part, :] * inverse), moved
        )
        moved = jnp.where(
            (kind == 2) | (kind == 3), jnp.minimum(moved, high_ref[part, :] * inverse), moved
        )
        shifted[part, :] = scale * (2.0 * moved - primal)
        primal_out[part, :] = scale * moved if last else moved

    def visit(slots, ids):
        return product_terms(shifted, [col for _, col in ids], [turned[slot] for slot in slots])

    def finish(row, col, term):
        add_row(row_acc, row_place(row, count, across), term, jnp.add)

    for_slots(ids_ref, visit, finish)
    store_pieces(row_acc, row_out, count)


def next_dual(first, image, inside, scale, demand, dual, dual_step):
    if first:
        dual = dual / scale
    row_image = scale * image[inside, :]
    return jnp.maximum(dual + dual_step * (scale * demand - row_image), 0.0)


def transposed_kernel(count, first, ids_ref, blocks, *refs):
    image, refs = refs[:2], refs[2:]
    scale_ref, demand_ref, dual_ref, cost_squares, demand_squares, dual_out = refs[:6]
    product_out, (weights, product_acc) = refs[6:10], refs[10:]
    mask, across = col_mask(), row_mask()
    size = count // CHUNKS
    product_acc[...] = jnp.zeros_like(product_acc)
    dual_step = STEP_SCALE * norm_ratio(cost_squares, demand_squares)
    for place in range(CHUNKS):
        part = chunk_rows(place ^ across, size)
        piece, inside = piece_chunk(image, place, size)
        scale = scale_ref[part, :]
        dual = next_dual(
            first, piece, inside, scale, demand_ref[part, :], dual_ref[part, :], dual_step
        )
        dual_out[part, :] = dual
        weights[part, :] = scale * dual

    def visit(slots, ids):
        return product_terms(weights, [row for row, _ in ids], [blocks[slot] for slot in slots])

    def finish(row, col, term):
        add_row(product_acc, col_place(col, count, mask), term, jnp.add)

    for_slots(ids_ref, visit, finish)
    store_pieces(product_acc, product_out, count)


def last_dual_kernel(count, first, *refs):
    image, refs = refs[:2], refs[2:]
    scale_ref, demand_ref, dual_ref, cost_squares, demand_squares, dual_out = refs
    across = row_mask()
    size = count // CHUNKS
    dual_step = STEP_SCALE * norm_ratio(cost_squares, demand_squares)
    for place in range(CHUNKS):
        part = chunk_rows(place ^ across, size)
        piece, inside = piece_chunk(image, place, size)
        scale = scale_ref[part, :]
        dual = next_dual(
            first, piece, inside, scale, demand_ref[part, :], dual_ref[part, :], dual_step
        )
        dual_out[part, :] = scale * dual


def vectors(*row_counts):
    return [jax.ShapeDtypeStruct((rows, 128), jnp.float32) for rows in row_counts]


def call_plain(kernel, operands, out_shape):
    return pl.pallas_call(
        kernel,
        out_shape=out_shape,
        in_specs=[pl.BlockSpec(memory_space=pltpu.VMEM)] * len(operands),
        out_specs=[pl.BlockSpec(memory_space=pltpu.VMEM)] * len(out_shape),
        compiler_params=pltpu.CompilerParams(vmem_limit_bytes=SMALL_VMEM),
    )(*operands)


def call_blocks(kernel, ids, values, operands, out_shape, scratch, first=False):
    width = values.shape[1]
    scratch_shapes = [pltpu.VMEM((rows, width), jnp.float32) for rows in scratch]
    if first:
        arrivals = pltpu.SemaphoreType.DMA((values.shape[0] // GROUP,))
        scratch_shapes = [arrivals] + scratch_shapes
    return pl.pallas_call(
        kernel,
        out_shape=out_shape,
        in_specs=[pl.BlockSpec(memory_space=pltpu.SMEM)]
        + [pl.BlockSpec(memory_space=pl.ANY if first else pltpu.VMEM)]
        + [pl.BlockSpec(memory_space=pltpu.VMEM)] * len(operands),
        out_specs=[pl.BlockSpec(memory_space=pltpu.VMEM)] * len(out_shape),
        scratch_shapes=scratch_shapes,
        compiler_params=pltpu.CompilerParams(
            vmem_limit_bytes=FIRST_VMEM if first else BLOCK_VMEM
        ),
        cost_estimate=pl.CostEstimate(
            flops=2 * values.size, bytes_accessed=2 * values.size, transcendentals=0
        ),
    )(ids, values, *operands)


def swap(vector, axis, size, bit):
    return lax.ppermute(vector, axis, [(i, i ^ bit) for i in range(size)])


def after(values, *earlier):
    return lax.optimization_barrier((values, earlier))[0]


def halve_rows(pieces, groups, combine):
    near, far = pieces
    return combine(near, swap(far, "col", groups, ROW_HALVING))


def exchange_rows(near, groups, combine):
    bit = 1
    while bit < groups:
        if bit != ROW_HALVING:
            near = combine(near, swap(near, "col", groups, bit))
        bit *= 2
    return near


def join_rows(near, groups):
    return [near, swap(near, "col", groups, ROW_HALVING)]


def scatter_cols(pieces, groups, combine, tie=()):
    diagonal = swap(pieces[3], "row", groups, 3)
    first, second = after((pieces[1], pieces[2]), *tie) if tie else pieces[1:3]
    first, second = swap(first, "row", groups, 1), swap(second, "row", groups, 2)
    return combine(combine(pieces[0], first), combine(second, diagonal))


def exchange_cols(piece, groups, combine):
    bit = QUARTERS
    while bit < groups:
        piece = combine(piece, swap(piece, "row", groups, bit))
        bit *= 2
    return piece


def gather_cols(piece, groups):
    diagonal = swap(piece, "row", groups, 3)
    return [piece, swap(piece, "row", groups, 1), swap(piece, "row", groups, 2), diagonal]


def sum_cols(vector, groups):
    bit = 1
    while bit < groups:
        vector = vector + swap(vector, "col", groups, bit)
        bit *= 2
    return vector


def per_device(
    row_groups,
    col_groups,
    block_values,
    block_rows,
    block_cols,
    cost_vec,
    demand,
    lower,
    upper,
    bound_kind,
    primal_start,
    dual_start,
):
    values = block_values[0, 0]
    width = values.shape[1]
    ids = jnp.concatenate([block_rows[0, 0], block_cols[0, 0]])
    row_length, col_length = demand.shape[0], cost_vec.shape[0]
    cost_vec, demand, lower, upper, bound_kind, primal_start, dual_start = [
        v.reshape(-1, width)
        for v in (cost_vec, demand, lower, upper, bound_kind, primal_start, dual_start)
    ]
    count = demand.shape[0]
    half, quarter, spare = count // 2, count // QUARTERS, count + 8
    row_pieces, col_pieces = vectors(half, half), vectors(*[quarter] * QUARTERS)
    whole = vectors(count)
    squares = vectors(8)

    def over_col(pieces, combine):
        near = exchange_rows(halve_rows(pieces, col_groups, combine), col_groups, combine)
        return join_rows(near, col_groups)

    def over_row(pieces, combine):
        share = scatter_cols(pieces, row_groups, combine)
        return gather_cols(exchange_cols(share, row_groups, combine), row_groups)

    tile = lax.broadcasted_iota(jnp.int32, (quarter + 8, width), 0)

    def mixed(a, b):
        return jnp.where(tile < quarter, jnp.maximum(a, b), a + b)

    block_shape = jax.ShapeDtypeStruct(values.shape, values.dtype)
    out = call_blocks(
        functools.partial(first_pass_kernel, count),
        ids,
        values,
        [],
        row_pieces + col_pieces + [block_shape],
        [spare] * 2,
        first=True,
    )
    blocks = out[6]
    near = halve_rows(out[:2], col_groups, jnp.maximum)
    *product_pieces, turned = call_blocks(
        functools.partial(first_product_kernel, count),
        ids,
        blocks,
        [after(dual_start, near)],
        col_pieces + [block_shape],
        [spare],
    )
    share = scatter_cols(out[2:6], row_groups, jnp.maximum, (near,))
    near = exchange_rows(near, col_groups, jnp.maximum)
    row_peaks = join_rows(near, col_groups)
    product = scatter_cols(after(product_pieces, near), row_groups, jnp.add)
    share = after(exchange_cols(share, row_groups, jnp.maximum), product_pieces)
    row_peaks, col_peaks = after((row_peaks, gather_cols(share, row_groups)), product)
    product = exchange_cols(product, row_groups, jnp.add)
    out = call_blocks(
        functools.partial(second_pass_kernel, count),
        ids,
        blocks,
        row_peaks + col_peaks,
        row_pieces + col_pieces + whole + whole,
        [spare] * 2,
    )
    row_scale, col_scale = out[6:]
    near = halve_rows(out[:2], col_groups, jnp.maximum)
    share = scatter_cols(out[2:6], row_groups, jnp.maximum, (near,))
    row_peaks = join_rows(exchange_rows(near, col_groups, jnp.maximum), col_groups)
    row_scale, demand_squares = call_plain(
        functools.partial(row_scale_kernel, count),
        row_peaks + [row_scale, demand],
        whole + squares,
    )
    share = after(jnp.concatenate([share, demand_squares], axis=0), product)
    product = gather_cols(after(product, share), row_groups)
    gathered = gather_cols(exchange_cols(share, row_groups, mixed), row_groups)
    col_scale, cost_squares, demand_squares = call_plain(
        functools.partial(col_scale_kernel, count),
        gathered + [col_scale, cost_vec],
        whole + squares + squares,
    )
    norms = [sum_cols(after(cost_squares, product), col_groups), demand_squares]

    def forward(first, last, product, primal):
        out = call_blocks(
            functools.partial(forward_kernel, count, first, last),
            ids,
            turned,
            product + [col_scale, cost_vec, lower, upper, bound_kind, primal] + norms,
            whole + row_pieces,
            [count, spare],
        )
        return out[0], over_col(out[1:], jnp.add)

    primal, image = forward(True, False, product, primal_start)
    out = call_blocks(
        functools.partial(transposed_kernel, count, True),
        ids,
        blocks,
        image + [row_scale, demand, dual_start] + norms,
        whole + col_pieces,
        [count, spare],
    )
    dual, product = out[0], over_row(out[1:], jnp.add)
    primal, image = forward(False, True, product, primal)
    (dual,) = call_plain(
        functools.partial(last_dual_kernel, count, False),
        image + [row_scale, demand, dual] + norms,
        whole,
    )
    return primal.reshape(col_length), dual.reshape(row_length)


def solution(mesh):
    def body(*args):
        return per_device(mesh.shape["row"], mesh.shape["col"], *args)

    return jax.shard_map(
        body,
        mesh=mesh,
        in_specs=(
            P("row", "col", None, None, None),
            P("row", "col", None),
            P("row", "col", None),
            P("col"),
            P("row"),
            P("col"),
            P("col"),
            P("col"),
            P("col"),
            P("row"),
        ),
        out_specs=(P("col"), P("row")),
        check_vma=False,
    )
```

profile of v0, /device:TPU:0, one launch (start us, length us, event | category | flops | bytes accessed | tf_op | source)
XLA Modules:
  0.0 120.0 jit_solution(13178612578837852953)
XLA Ops:
  0.6 0.7 pad_add_fusion.ids_ref
  1.4 5.6 %shard_map.113 = (f32[256,128]{1,0:T(8,128)S(1)}, f32[256,128]{1,0:T(8,128)S(1)}, f32[128,128]{1,0:T(8,128)S(1)}, f32[128,128]{1,0:T(8,128)S(1)}, f32[128,128]{1...) custom-call(s32[512]{0:T(512)S(1)} %pad_add_fusion.ids_ref, bf16[256,128,128]{2,1,0:T(8,128)(2,1)} %bitcast.27), custom_call_target="tpu_custom_call" | custom-call | flops 8388608 | bytes 8388608 | tf_op jit(solution)/shard_map/pallas_call | solution.py:373
  7.0 0.5 collective-permute-start
  7.6 3.6 %collective-permute-start.9 = (f32[128,128]{1,0:T(8,128)S(1)}, f32[128,128]{1,0:T(8,128)S(1)}, u32[]{:S(2)}, u32[]{:S(2)}) collective-permute-start(f32[128,128]{1,0:T(8,128)S(1)} %get-tuple-element.75), channel_id=1, source_target_pairs={{0,12},{4,8},{8,4},{12,0},{16,28},{20,24},{24,20},{28,16},{1,13},{... | collective-permute-start | bytes 196616 | tf_op jit(solution)/shard_map/ppermute | solution.py:391
  11.1 0.6 collective-permute-start.8
  11.8 1.3 %collective-permute-start.7 = (f32[128,128]{1,0:T(8,128)S(1)}, f32[128,128]{1,0:T(8,128)S(1)}, u32[]{:S(2)}, u32[]{:S(2)}) collective-permute-start(f32[128,128]{1,0:T(8,128)S(1)} %get-tuple-element.73), channel_id=1, source_target_pairs={{0,4},{4,0},{8,12},{12,8},{16,20},{20,16},{24,28},{28,24},{1,5},{5... | collective-permute-start | bytes 196616 | tf_op jit(solution)/shard_map/ppermute | solution.py:391
  13.0 1.6 %collective-permute-start.1 = (f32[256,128]{1,0:T(8,128)S(1)}, f32[256,128]{1,0:T(8,128)S(1)}, u32[]{:S(2)}, u32[]{:S(2)}) collective-permute-start(f32[256,128]{1,0:T(8,128)S(1)} %max.36), channel_id=1, source_target_pairs={{0,2},{1,3},{2,0},{3,1},{4,6},{5,7},{6,4},{7,5},{8,10},{9,11},{10,... | collective-permute-start | bytes 393224 | tf_op jit(solution)/shard_map/ppermute | solution.py:391
  14.6 3.3 %shard_map.114 = (f32[128,128]{1,0:T(8,128)S(1)}, f32[128,128]{1,0:T(8,128)S(1)}, f32[128,128]{1,0:T(8,128)S(1)}, f32[128,128]{1,0:T(8,128)S(1)}, bf16[256,128,128]{2,1,0:T(8,128)(2,1)S(1)}) custom-call(s32[512]{0:T(512)S(1)} %pad_add_fusion.ids_ref, bf16[256,128,128]{2,1,0:T(8,128)(2,1)S(1)} %get-tuple-element.57.blocks, f32[512,128]{1,0:T(8,128)S(1)} %bitcast.18), custom_call_target="tpu_custom_call" | custom-call | flops 8388608 | bytes 8388608 | tf_op jit(solution)/shard_map/pallas_call | solution.py:373
  18.1 2.6 %collective-permute-start.10 = (f32[128,128]{1,0:T(8,128)S(1)}, f32[128,128]{1,0:T(8,128)S(1)}, u32[]{:S(2)}, u32[]{:S(2)}) collective-permute-start(f32[128,128]{1,0:T(8,128)S(1)} %maximum_maximum_fusion.1), channel_id=1, source_target_pairs={{0,16},{4,20},{8,24},{12,28},{16,0},{20,4},{24,8},{28,12},{1,17},{... | collective-permute-start | bytes 196616 | tf_op jit(solution)/shard_map/ppermute | solution.py:391
  20.7 0.8 collective-permute-start.3
  21.6 1.3 %collective-permute-start.4 = (f32[128,128]{1,0:T(8,128)S(1)}, f32[128,128]{1,0:T(8,128)S(1)}, u32[]{:S(2)}, u32[]{:S(2)}) collective-permute-start(f32[128,128]{1,0:T(8,128)S(1)} %get-tuple-element.69), channel_id=1, source_target_pairs={{0,12},{4,8},{8,4},{12,0},{16,28},{20,24},{24,20},{28,16},{1,13},{... | collective-permute-start | bytes 196616 | tf_op jit(solution)/shard_map/ppermute | solution.py:391
  22.9 1.4 %collective-permute-start.2 = (f32[128,128]{1,0:T(8,128)S(1)}, f32[128,128]{1,0:T(8,128)S(1)}, u32[]{:S(2)}, u32[]{:S(2)}) collective-permute-start(f32[128,128]{1,0:T(8,128)S(1)} %get-tuple-element.67), channel_id=1, source_target_pairs={{0,4},{4,0},{8,12},{12,8},{16,20},{20,16},{24,28},{28,24},{1,5},{5... | collective-permute-start | bytes 196616 | tf_op jit(solution)/shard_map/ppermute | solution.py:391
  24.3 0.7 collective-permute-start.11
  25.4 1.1 collective-permute-start.12
  26.8 1.3 %collective-permute-start.13 = (f32[128,128]{1,0:T(8,128)S(1)}, f32[128,128]{1,0:T(8,128)S(1)}, u32[]{:S(2)}, u32[]{:S(2)}) collective-permute-start(f32[128,128]{1,0:T(8,128)S(1)} %max.41.refs_2_), channel_id=1, source_target_pairs={{0,12},{4,8},{8,4},{12,0},{16,28},{20,24},{24,20},{28,16},{1,13},{... | collective-permute-start | bytes 196616 | tf_op jit(solution)/shard_map/ppermute | solution.py:391
  28.1 0.8 collective-permute-done.11.refs_3_
  28.9 1.3 %collective-permute-done.12.refs_4_ = f32[128,128]{1,0:T(8,128)S(1)} collective-permute-done((f32[128,128]{1,0:T(8,128)S(1)}, f32[128,128]{1,0:T(8,128)S(1)}, u32[]{:S(2)}, u32[]{:S(2)}) %collective-permute-start.12) | collective-permute-done | bytes 65568 | tf_op jit(solution)/shard_map/ppermute | solution.py:391
  30.2 1.7 %collective-permute-done.13.refs_5_ = f32[128,128]{1,0:T(8,128)S(1)} collective-permute-done((f32[128,128]{1,0:T(8,128)S(1)}, f32[128,128]{1,0:T(8,128)S(1)}, u32[]{:S(2)}, u32[]{:S(2)}) %collective-permute-start.13) | collective-permute-done | bytes 65568 | tf_op jit(solution)/shard_map/ppermute | solution.py:391
  31.9 7.7 %shard_map.115 = (f32[256,128]{1,0:T(8,128)S(1)}, f32[256,128]{1,0:T(8,128)S(1)}, f32[128,128]{1,0:T(8,128)S(1)}, f32[128,128]{1,0:T(8,128)S(1)}, f32[128,128]{1...) custom-call(s32[512]{0:T(512)S(1)} %pad_add_fusion.ids_ref, ...), custom_call_target="tpu_custom_call" | custom-call | flops 8388608 | bytes 8388608 | tf_op jit(solution)/shard_map/pallas_call | solution.py:373
  39.7 1.3 %collective-permute-done.14 = f32[256,128]{1,0:T(8,128)S(1)} collective-permute-done((f32[256,128]{1,0:T(8,128)S(1)}, f32[256,128]{1,0:T(8,128)S(1)}, u32[]{:S(2)}, u32[]{:S(2)}) %collective-permute-start.14) | collective-permute-done | bytes 131104 | tf_op jit(solution)/shard_map/ppermute | solution.py:391
  41.6 2.1 %collective-permute-start.5 = (f32[128,128]{1,0:T(8,128)S(1)}, f32[128,128]{1,0:T(8,128)S(1)}, u32[]{:S(2)}, u32[]{:S(2)}) collective-permute-start(f32[128,128]{1,0:T(8,128)S(1)} %add_add_fusion.1), channel_id=1, source_target_pairs={{0,16},{4,20},{8,24},{12,28},{16,0},{20,4},{24,8},{28,12},{1,17},{... | collective-permute-start | bytes 196616 | tf_op jit(solution)/shard_map/ppermute | solution.py:391
  43.6 1.2 %collective-permute-start.17 = (f32[128,128]{1,0:T(8,128)S(1)}, f32[128,128]{1,0:T(8,128)S(1)}, u32[]{:S(2)}, u32[]{:S(2)}) collective-permute-start(f32[128,128]{1,0:T(8,128)S(1)} %get-tuple-element.90), channel_id=1, source_target_pairs={{0,12},{4,8},{8,4},{12,0},{16,28},{20,24},{24,20},{28,16},{1,13},{... | collective-permute-start | bytes 196616 | tf_op jit(solution)/shard_map/ppermute | solution.py:391
  44.8 0.6 collective-permute-start.16
  45.5 1.6 %collective-permute-start.15 = (f32[128,128]{1,0:T(8,128)S(1)}, f32[128,128]{1,0:T(8,128)S(1)}, u32[]{:S(2)}, u32[]{:S(2)}) collective-permute-start(f32[128,128]{1,0:T(8,128)S(1)} %get-tuple-element.88), channel_id=1, source_target_pairs={{0,4},{4,0},{8,12},{12,8},{16,20},{20,16},{24,28},{28,24},{1,5},{5... | collective-permute-start | bytes 196616 | tf_op jit(solution)/shard_map/ppermute | solution.py:391
  47.1 0.6 collective-permute-done.5
  47.8 2.2 %collective-permute-done.17 = f32[128,128]{1,0:T(8,128)S(1)} collective-permute-done((f32[128,128]{1,0:T(8,128)S(1)}, f32[128,128]{1,0:T(8,128)S(1)}, u32[]{:S(2)}, u32[]{:S(2)}) %collective-permute-start.17) | collective-permute-done | bytes 65568 | tf_op jit(solution)/shard_map/ppermute | solution.py:391
  50.4 1.5 %collective-permute-start.23 = (f32[136,128]{1,0:T(8,128)S(1)}, f32[136,128]{1,0:T(8,128)S(1)}, u32[]{:S(2)}, u32[]{:S(2)}) collective-permute-start(f32[136,128]{1,0:T(8,128)S(1)} %pad_maximum_fusion), channel_id=1, source_target_pairs={{0,16},{4,20},{8,24},{12,28},{16,0},{20,4},{24,8},{28,12},{1,17},{... | collective-permute-start | bytes 208904 | tf_op jit(solution)/shard_map/ppermute | solution.py:391
  51.9 4.5 %collective-permute-done.23 = f32[136,128]{1,0:T(8,128)S(1)} collective-permute-done((f32[136,128]{1,0:T(8,128)S(1)}, f32[136,128]{1,0:T(8,128)S(1)}, u32[]{:S(2)}, u32[]{:S(2)}) %collective-permute-start.23) | collective-permute-done | bytes 69664 | tf_op jit(solution)/shard_map/ppermute | solution.py:391
  56.5 1.2 %collective-permute-start.24 = (f32[136,128]{1,0:T(8,128)S(1)}, f32[136,128]{1,0:T(8,128)S(1)}, u32[]{:S(2)}, u32[]{:S(2)}) collective-permute-start(f32[136,128]{1,0:T(8,128)S(1)} %add_select_fusion.refs_0_), channel_id=1, source_target_pairs={{0,4},{4,0},{8,12},{12,8},{16,20},{20,16},{24,28},{28,24},{1,5},{5... | collective-permute-start | bytes 208904 | tf_op jit(solution)/shard_map/ppermute | solution.py:391
  57.7 2.3 %collective-permute-start.26 = (f32[136,128]{1,0:T(8,128)S(1)}, f32[136,128]{1,0:T(8,128)S(1)}, u32[]{:S(2)}, u32[]{:S(2)}) collective-permute-start(f32[136,128]{1,0:T(8,128)S(1)} %add_select_fusion.refs_0_), channel_id=1, source_target_pairs={{0,12},{4,8},{8,4},{12,0},{16,28},{20,24},{24,20},{28,16},{1,13},{... | collective-permute-start | bytes 208904 | tf_op jit(solution)/shard_map/ppermute | solution.py:391
  60.0 1.2 collective-permute-start.20
  61.2 2.3 %collective-permute-start.22 = (f32[128,128]{1,0:T(8,128)S(1)}, f32[128,128]{1,0:T(8,128)S(1)}, u32[]{:S(2)}, u32[]{:S(2)}) collective-permute-start(f32[128,128]{1,0:T(8,128)S(1)} %add.48.refs_0_), channel_id=1, source_target_pairs={{0,12},{4,8},{8,4},{12,0},{16,28},{20,24},{24,20},{28,16},{1,13},{... | collective-permute-start | bytes 196616 | tf_op jit(solution)/shard_map/ppermute | solution.py:391
  63.9 0.6 collective-permute-done.20.refs_1_
  64.5 1.0 collective-permute-done.21.refs_2_
  65.5 1.0 collective-permute-done.22.refs_3_
  66.5 1.2 collective-permute-done.27
  67.6 1.5 %collective-permute-start.28 = (f32[8,128]{1,0:T(8,128)S(1)}, f32[8,128]{1,0:T(8,128)S(1)}, u32[]{:S(2)}, u32[]{:S(2)}) collective-permute-start(f32[8,128]{1,0:T(8,128)S(1)} %add.50), channel_id=1, source_target_pairs={{0,2},{1,3},{2,0},{3,1},{4,6},{5,7},{6,4},{7,5},{8,10},{9,11},{10,... | collective-permute-start | bytes 12296 | tf_op jit(solution)/shard_map/ppermute | solution.py:391
  69.2 2.1 %collective-permute-done.28 = f32[8,128]{1,0:T(8,128)S(1)} collective-permute-done((f32[8,128]{1,0:T(8,128)S(1)}, f32[8,128]{1,0:T(8,128)S(1)}, u32[]{:S(2)}, u32[]{:S(2)}) %collective-permute-start.28) | collective-permute-done | bytes 4128 | tf_op jit(solution)/shard_map/ppermute | solution.py:391
  71.3 3.3 %shard_map.118 = (f32[512,128]{1,0:T(8,128)S(1)}, f32[256,128]{1,0:T(8,128)S(1)}, f32[256,128]{1,0:T(8,128)S(1)}) custom-call(s32[512]{0:T(512)S(1)} %pad_add_fusion.ids_ref, bf16[256,128,128]{2,1,0:T(8,128)(2,1)S(1)} %get-tuple-element.61.turned, f32[128,128]{1,0:T(8,128)S(1)} %add.48.refs_0_, f32[128,128]{1,0:T(8,128)S(1)} %collective-permute-done.20.refs_1_, ...), custom_call_target="tpu_custom_call" | custom-call | flops 8388608 | bytes 8388608 | tf_op jit(solution)/shard_map/pallas_call | solution.py:373
  74.6 1.3 %collective-permute-done.29 = f32[256,128]{1,0:T(8,128)S(1)} collective-permute-done((f32[256,128]{1,0:T(8,128)S(1)}, f32[256,128]{1,0:T(8,128)S(1)}, u32[]{:S(2)}, u32[]{:S(2)}) %collective-permute-start.29) | collective-permute-done | bytes 131104 | tf_op jit(solution)/shard_map/ppermute | solution.py:391
  76.0 1.5 %collective-permute-start.30 = (f32[256,128]{1,0:T(8,128)S(1)}, f32[256,128]{1,0:T(8,128)S(1)}, u32[]{:S(2)}, u32[]{:S(2)}) collective-permute-start(f32[256,128]{1,0:T(8,128)S(1)} %add.52), channel_id=1, source_target_pairs={{0,2},{1,3},{2,0},{3,1},{4,6},{5,7},{6,4},{7,5},{8,10},{9,11},{10,... | collective-permute-start | bytes 393224 | tf_op jit(solution)/shard_map/ppermute | solution.py:391
  77.5 4.2 %collective-permute-done.30 = f32[256,128]{1,0:T(8,128)S(1)} collective-permute-done((f32[256,128]{1,0:T(8,128)S(1)}, f32[256,128]{1,0:T(8,128)S(1)}, u32[]{:S(2)}, u32[]{:S(2)}) %collective-permute-start.30) | collective-permute-done | bytes 131104 | tf_op jit(solution)/shard_map/ppermute | solution.py:391
  81.7 1.3 %collective-permute-done.31.refs_1_ = f32[256,128]{1,0:T(8,128)S(1)} collective-permute-done((f32[256,128]{1,0:T(8,128)S(1)}, f32[256,128]{1,0:T(8,128)S(1)}, u32[]{:S(2)}, u32[]{:S(2)}) %collective-permute-start.31) | collective-permute-done | bytes 131104 | tf_op jit(solution)/shard_map/ppermute | solution.py:391
  83.1 3.2 %shard_map.119 = (f32[512,128]{1,0:T(8,128)S(1)}, f32[128,128]{1,0:T(8,128)S(1)}, f32[128,128]{1,0:T(8,128)S(1)}, f32[128,128]{1,0:T(8,128)S(1)}, f32[128,128]{1,0:T(8,128)S(1)}) custom-call(s32[512]{0:T(512)S(1)} %pad_add_fusion.ids_ref, bf16[256,128,128]{2,1,0:T(8,128)(2,1)S(1)} %get-tuple-element.57.blocks, f32[256,128]{1,0:T(8,128)S(1)} %add.53.refs_0_, ...), custom_call_target="tpu_custom_call" | custom-call | flops 8388608 | bytes 8388608 | tf_op jit(solution)/shard_map/pallas_call | solution.py:373
  86.2 2.0 %collective-permute-start.33 = (f32[128,128]{1,0:T(8,128)S(1)}, f32[128,128]{1,0:T(8,128)S(1)}, u32[]{:S(2)}, u32[]{:S(2)}) collective-permute-start(f32[128,128]{1,0:T(8,128)S(1)} %get-tuple-element.105), channel_id=1, source_target_pairs={{0,8},{4,12},{8,0},{12,4},{16,24},{20,28},{24,16},{28,20},{1,9},{5... | collective-permute-start | bytes 196616 | tf_op jit(solution)/shard_map/ppermute | solution.py:391
  88.3 1.0 collective-permute-start.34
  89.3 0.5 collective-permute-start.32
  89.8 0.8 collective-permute-done.33
  90.6 2.9 %collective-permute-done.34 = f32[128,128]{1,0:T(8,128)S(1)} collective-permute-done((f32[128,128]{1,0:T(8,128)S(1)}, f32[128,128]{1,0:T(8,128)S(1)}, u32[]{:S(2)}, u32[]{:S(2)}) %collective-permute-start.34) | collective-permute-done | bytes 65568 | tf_op jit(solution)/shard_map/ppermute | solution.py:391
  93.5 0.6 collective-permute-done.32
  94.1 1.4 %collective-permute-start.35 = (f32[128,128]{1,0:T(8,128)S(1)}, f32[128,128]{1,0:T(8,128)S(1)}, u32[]{:S(2)}, u32[]{:S(2)}) collective-permute-start(f32[128,128]{1,0:T(8,128)S(1)} %add_add_fusion), channel_id=1, source_target_pairs={{0,16},{4,20},{8,24},{12,28},{16,0},{20,4},{24,8},{28,12},{1,17},{... | collective-permute-start | bytes 196616 | tf_op jit(solution)/shard_map/ppermute | solution.py:391
  95.5 4.6 %collective-permute-done.35 = f32[128,128]{1,0:T(8,128)S(1)} collective-permute-done((f32[128,128]{1,0:T(8,128)S(1)}, f32[128,128]{1,0:T(8,128)S(1)}, u32[]{:S(2)}, u32[]{:S(2)}) %collective-permute-start.35) | collective-permute-done | bytes 65568 | tf_op jit(solution)/shard_map/ppermute | solution.py:391
  100.1 0.9 collective-permute-start.36
  101.0 0.6 collective-permute-start.37
  101.5 2.1 %collective-permute-start.38 = (f32[128,128]{1,0:T(8,128)S(1)}, f32[128,128]{1,0:T(8,128)S(1)}, u32[]{:S(2)}, u32[]{:S(2)}) collective-permute-start(f32[128,128]{1,0:T(8,128)S(1)} %add.57.refs_0_), channel_id=1, source_target_pairs={{0,12},{4,8},{8,4},{12,0},{16,28},{20,24},{24,20},{28,16},{1,13},{... | collective-permute-start | bytes 196616 | tf_op jit(solution)/shard_map/ppermute | solution.py:391
  103.6 0.8 collective-permute-done.36.refs_1_
  104.4 0.8 collective-permute-done.37.refs_2_
  105.2 1.5 %collective-permute-done.38.refs_3_ = f32[128,128]{1,0:T(8,128)S(1)} collective-permute-done((f32[128,128]{1,0:T(8,128)S(1)}, f32[128,128]{1,0:T(8,128)S(1)}, u32[]{:S(2)}, u32[]{:S(2)}) %collective-permute-start.38) | collective-permute-done | bytes 65568 | tf_op jit(solution)/shard_map/ppermute | solution.py:391
  106.7 3.9 %shard_map.120 = (f32[512,128]{1,0:T(8,128)}, f32[256,128]{1,0:T(8,128)S(1)}, f32[256,128]{1,0:T(8,128)S(1)}) custom-call(s32[512]{0:T(512)S(1)} %pad_add_fusion.ids_ref, bf16[256,128,128]{2,1,0:T(8,128)(2,1)S(1)} %get-tuple-element.61.turned, f32[128,128]{1,0:T(8,128)S(1)} %add.57.refs_0_, f32[128,128]{1,0:T(8,128)S(1)} %collective-permute-done.36.refs_1_, ...), custom_call_target="tpu_custom_call" | custom-call | flops 8388608 | bytes 8388608 | tf_op jit(solution)/shard_map/pallas_call | solution.py:373
  110.6 1.3 %collective-permute-done.39 = f32[256,128]{1,0:T(8,128)S(1)} collective-permute-done((f32[256,128]{1,0:T(8,128)S(1)}, f32[256,128]{1,0:T(8,128)S(1)}, u32[]{:S(2)}, u32[]{:S(2)}) %collective-permute-start.39) | collective-permute-done | bytes 131104 | tf_op jit(solution)/shard_map/ppermute | solution.py:391
  112.0 1.9 %collective-permute-start.40 = (f32[256,128]{1,0:T(8,128)S(1)}, f32[256,128]{1,0:T(8,128)S(1)}, u32[]{:S(2)}, u32[]{:S(2)}) collective-permute-start(f32[256,128]{1,0:T(8,128)S(1)} %add.58), channel_id=1, source_target_pairs={{0,2},{1,3},{2,0},{3,1},{4,6},{5,7},{6,4},{7,5},{8,10},{9,11},{10,... | collective-permute-start | bytes 393224 | tf_op jit(solution)/shard_map/ppermute | solution.py:391
  113.9 3.8 %collective-permute-done.40 = f32[256,128]{1,0:T(8,128)S(1)} collective-permute-done((f32[256,128]{1,0:T(8,128)S(1)}, f32[256,128]{1,0:T(8,128)S(1)}, u32[]{:S(2)}, u32[]{:S(2)}) %collective-permute-start.40) | collective-permute-done | bytes 131104 | tf_op jit(solution)/shard_map/ppermute | solution.py:391
  117.8 1.3 %collective-permute-done.41.refs_1_ = f32[256,128]{1,0:T(8,128)S(1)} collective-permute-done((f32[256,128]{1,0:T(8,128)S(1)}, f32[256,128]{1,0:T(8,128)S(1)}, u32[]{:S(2)}, u32[]{:S(2)}) %collective-permute-start.41) | collective-permute-done | bytes 131104 | tf_op jit(solution)/shard_map/ppermute | solution.py:391
  119.1 0.9 shard_map.121
  (64 shorter events, 2.5 us)
Async XLA Ops:
  0.6 14.0 %copy-start.2 = (f32[65536]{0:T(1024)S(1)}, f32[65536]{0:T(1024)}, u32[]{:S(2)}) copy-start(f32[65536]{0:T(1024)} %param.19) | copy-start | bytes 786436
  7.0 4.1 %collective-permute-start = (f32[256,128]{1,0:T(8,128)S(1)}, f32[256,128]{1,0:T(8,128)S(1)}, u32[]{:S(2)}, u32[]{:S(2)}) collective-permute-start(f32[256,128]{1,0:T(8,128)S(1)} %get-tuple-element.59), channel_id=1, source_target_pairs={{0,1},{1,0},{2,3},{3,2},{4,5},{5,4},{6,7},{7,6},{8,9},{9,8},{10,11... | collective-permute-start | bytes 393224 | tf_op jit(solution)/shard_map/ppermute | solution.py:391
  7.6 10.5 %collective-permute-start.9 = (f32[128,128]{1,0:T(8,128)S(1)}, f32[128,128]{1,0:T(8,128)S(1)}, u32[]{:S(2)}, u32[]{:S(2)}) collective-permute-start(f32[128,128]{1,0:T(8,128)S(1)} %get-tuple-element.75), channel_id=1, source_target_pairs={{0,12},{4,8},{8,4},{12,0},{16,28},{20,24},{24,20},{28,16},{1,13},{... | collective-permute-start | bytes 196616 | tf_op jit(solution)/shard_map/ppermute | solution.py:391
  11.1 6.9 %collective-permute-start.8 = (f32[128,128]{1,0:T(8,128)S(1)}, f32[128,128]{1,0:T(8,128)S(1)}, u32[]{:S(2)}, u32[]{:S(2)}) collective-permute-start(f32[128,128]{1,0:T(8,128)S(1)} %get-tuple-element.74), channel_id=1, source_target_pairs={{0,8},{4,12},{8,0},{12,4},{16,24},{20,28},{24,16},{28,20},{1,9},{5... | collective-permute-start | bytes 196616 | tf_op jit(solution)/shard_map/ppermute | solution.py:391
  11.8 6.3 %collective-permute-start.7 = (f32[128,128]{1,0:T(8,128)S(1)}, f32[128,128]{1,0:T(8,128)S(1)}, u32[]{:S(2)}, u32[]{:S(2)}) collective-permute-start(f32[128,128]{1,0:T(8,128)S(1)} %get-tuple-element.73), channel_id=1, source_target_pairs={{0,4},{4,0},{8,12},{12,8},{16,20},{20,16},{24,28},{28,24},{1,5},{5... | collective-permute-start | bytes 196616 | tf_op jit(solution)/shard_map/ppermute | solution.py:391
  13.0 7.7 %collective-permute-start.1 = (f32[256,128]{1,0:T(8,128)S(1)}, f32[256,128]{1,0:T(8,128)S(1)}, u32[]{:S(2)}, u32[]{:S(2)}) collective-permute-start(f32[256,128]{1,0:T(8,128)S(1)} %max.36), channel_id=1, source_target_pairs={{0,2},{1,3},{2,0},{3,1},{4,6},{5,7},{6,4},{7,5},{8,10},{9,11},{10,... | collective-permute-start | bytes 393224 | tf_op jit(solution)/shard_map/ppermute | solution.py:391
  14.6 35.6 %copy-start.1 = (f32[65536]{0:T(1024)S(1)}, f32[65536]{0:T(1024)}, u32[]{:S(2)}) copy-start(f32[65536]{0:T(1024)} %param.14) | copy-start | bytes 786436
  18.0 45.8 %copy-start = (f32[65536]{0:T(1024)S(1)}, f32[65536]{0:T(1024)}, u32[]{:S(2)}) copy-start(f32[65536]{0:T(1024)} %param.13) | copy-start | bytes 786436
  18.0 53.3 %copy-start.3 = (f32[65536]{0:T(1024)S(1)}, f32[65536]{0:T(1024)}, u32[]{:S(2)}) copy-start(f32[65536]{0:T(1024)} %param.15) | copy-start | bytes 786436
  18.0 53.3 %copy-start.4 = (f32[65536]{0:T(1024)S(1)}, f32[65536]{0:T(1024)}, u32[]{:S(2)}) copy-start(f32[65536]{0:T(1024)} %param.16) | copy-start | bytes 786436
  18.0 53.3 %copy-start.5 = (s32[65536]{0:T(1024)S(1)}, s32[65536]{0:T(1024)}, u32[]{:S(2)}) copy-start(s32[65536]{0:T(1024)} %param.17) | copy-start | bytes 786436
  18.0 53.3 %copy-start.6 = (f32[65536]{0:T(1024)S(1)}, f32[65536]{0:T(1024)}, u32[]{:S(2)}) copy-start(f32[65536]{0:T(1024)} %param.18) | copy-start | bytes 786436
  18.1 6.2 %collective-permute-start.10 = (f32[128,128]{1,0:T(8,128)S(1)}, f32[128,128]{1,0:T(8,128)S(1)}, u32[]{:S(2)}, u32[]{:S(2)}) collective-permute-start(f32[128,128]{1,0:T(8,128)S(1)} %maximum_maximum_fusion.1), channel_id=1, source_target_pairs={{0,16},{4,20},{8,24},{12,28},{16,0},{20,4},{24,8},{28,12},{1,17},{... | collective-permute-start | bytes 196616 | tf_op jit(solution)/shard_map/ppermute | solution.py:391
  20.7 4.7 %collective-permute-start.3 = (f32[128,128]{1,0:T(8,128)S(1)}, f32[128,128]{1,0:T(8,128)S(1)}, u32[]{:S(2)}, u32[]{:S(2)}) collective-permute-start(f32[128,128]{1,0:T(8,128)S(1)} %get-tuple-element.68), channel_id=1, source_target_pairs={{0,8},{4,12},{8,0},{12,4},{16,24},{20,28},{24,16},{28,20},{1,9},{5... | collective-permute-start | bytes 196616 | tf_op jit(solution)/shard_map/ppermute | solution.py:391
  21.6 5.2 %collective-permute-start.4 = (f32[128,128]{1,0:T(8,128)S(1)}, f32[128,128]{1,0:T(8,128)S(1)}, u32[]{:S(2)}, u32[]{:S(2)}) collective-permute-start(f32[128,128]{1,0:T(8,128)S(1)} %get-tuple-element.69), channel_id=1, source_target_pairs={{0,12},{4,8},{8,4},{12,0},{16,28},{20,24},{24,20},{28,16},{1,13},{... | collective-permute-start | bytes 196616 | tf_op jit(solution)/shard_map/ppermute | solution.py:391
  22.9 5.2 %collective-permute-start.2 = (f32[128,128]{1,0:T(8,128)S(1)}, f32[128,128]{1,0:T(8,128)S(1)}, u32[]{:S(2)}, u32[]{:S(2)}) collective-permute-start(f32[128,128]{1,0:T(8,128)S(1)} %get-tuple-element.67), channel_id=1, source_target_pairs={{0,4},{4,0},{8,12},{12,8},{16,20},{20,16},{24,28},{28,24},{1,5},{5... | collective-permute-start | bytes 196616 | tf_op jit(solution)/shard_map/ppermute | solution.py:391
  24.3 7.7 %collective-permute-start.6 = (f32[256,128]{1,0:T(8,128)S(1)}, f32[256,128]{1,0:T(8,128)S(1)}, u32[]{:S(2)}, u32[]{:S(2)}) collective-permute-start(f32[256,128]{1,0:T(8,128)S(1)} %max.37.refs_0_), channel_id=1, source_target_pairs={{0,1},{1,0},{2,3},{3,2},{4,5},{5,4},{6,7},{7,6},{8,9},{9,8},{10,11... | collective-permute-start | bytes 393224 | tf_op jit(solution)/shard_map/ppermute | solution.py:391
  24.3 4.6 %collective-permute-start.11 = (f32[128,128]{1,0:T(8,128)S(1)}, f32[128,128]{1,0:T(8,128)S(1)}, u32[]{:S(2)}, u32[]{:S(2)}) collective-permute-start(f32[128,128]{1,0:T(8,128)S(1)} %max.41.refs_2_), channel_id=1, source_target_pairs={{0,4},{4,0},{8,12},{12,8},{16,20},{20,16},{24,28},{28,24},{1,5},{5... | collective-permute-start | bytes 196616 | tf_op jit(solution)/shard_map/ppermute | solution.py:391
  25.4 4.8 %collective-permute-start.12 = (f32[128,128]{1,0:T(8,128)S(1)}, f32[128,128]{1,0:T(8,128)S(1)}, u32[]{:S(2)}, u32[]{:S(2)}) collective-permute-start(f32[128,128]{1,0:T(8,128)S(1)} %max.41.refs_2_), channel_id=1, source_target_pairs={{0,8},{4,12},{8,0},{12,4},{16,24},{20,28},{24,16},{28,20},{1,9},{5... | collective-permute-start | bytes 196616 | tf_op jit(solution)/shard_map/ppermute | solution.py:391
  26.8 5.2 %collective-permute-start.13 = (f32[128,128]{1,0:T(8,128)S(1)}, f32[128,128]{1,0:T(8,128)S(1)}, u32[]{:S(2)}, u32[]{:S(2)}) collective-permute-start(f32[128,128]{1,0:T(8,128)S(1)} %max.41.refs_2_), channel_id=1, source_target_pairs={{0,12},{4,8},{8,4},{12,0},{16,28},{20,24},{24,20},{28,16},{1,13},{... | collective-permute-start | bytes 196616 | tf_op jit(solution)/shard_map/ppermute | solution.py:391
  39.6 1.4 %collective-permute-start.14 = (f32[256,128]{1,0:T(8,128)S(1)}, f32[256,128]{1,0:T(8,128)S(1)}, u32[]{:S(2)}, u32[]{:S(2)}) collective-permute-start(f32[256,128]{1,0:T(8,128)S(1)} %get-tuple-element.87), channel_id=1, source_target_pairs={{0,1},{1,0},{2,3},{3,2},{4,5},{5,4},{6,7},{7,6},{8,9},{9,8},{10,11... | collective-permute-start | bytes 393224 | tf_op jit(solution)/shard_map/ppermute | solution.py:391
  41.1 6.7 %collective-permute-start.18 = (f32[256,128]{1,0:T(8,128)S(1)}, f32[256,128]{1,0:T(8,128)S(1)}, u32[]{:S(2)}, u32[]{:S(2)}) collective-permute-start(f32[256,128]{1,0:T(8,128)S(1)} %max.42), channel_id=1, source_target_pairs={{0,2},{1,3},{2,0},{3,1},{4,6},{5,7},{6,4},{7,5},{8,10},{9,11},{10,... | collective-permute-start | bytes 393224 | tf_op jit(solution)/shard_map/ppermute | solution.py:391
  41.6 6.2 %collective-permute-start.5 = (f32[128,128]{1,0:T(8,128)S(1)}, f32[128,128]{1,0:T(8,128)S(1)}, u32[]{:S(2)}, u32[]{:S(2)}) collective-permute-start(f32[128,128]{1,0:T(8,128)S(1)} %add_add_fusion.1), channel_id=1, source_target_pairs={{0,16},{4,20},{8,24},{12,28},{16,0},{20,4},{24,8},{28,12},{1,17},{... | collective-permute-start | bytes 196616 | tf_op jit(solution)/shard_map/ppermute | solution.py:391
  43.6 6.5 %collective-permute-start.17 = (f32[128,128]{1,0:T(8,128)S(1)}, f32[128,128]{1,0:T(8,128)S(1)}, u32[]{:S(2)}, u32[]{:S(2)}) collective-permute-start(f32[128,128]{1,0:T(8,128)S(1)} %get-tuple-element.90), channel_id=1, source_target_pairs={{0,12},{4,8},{8,4},{12,0},{16,28},{20,24},{24,20},{28,16},{1,13},{... | collective-permute-start | bytes 196616 | tf_op jit(solution)/shard_map/ppermute | solution.py:391
  44.8 5.2 %collective-permute-start.16 = (f32[128,128]{1,0:T(8,128)S(1)}, f32[128,128]{1,0:T(8,128)S(1)}, u32[]{:S(2)}, u32[]{:S(2)}) collective-permute-start(f32[128,128]{1,0:T(8,128)S(1)} %get-tuple-element.89), channel_id=1, source_target_pairs={{0,8},{4,12},{8,0},{12,4},{16,24},{20,28},{24,16},{28,20},{1,9},{5... | collective-permute-start | bytes 196616 | tf_op jit(solution)/shard_map/ppermute | solution.py:391
  45.5 4.7 %collective-permute-start.15 = (f32[128,128]{1,0:T(8,128)S(1)}, f32[128,128]{1,0:T(8,128)S(1)}, u32[]{:S(2)}, u32[]{:S(2)}) collective-permute-start(f32[128,128]{1,0:T(8,128)S(1)} %get-tuple-element.88), channel_id=1, source_target_pairs={{0,4},{4,0},{8,12},{12,8},{16,20},{20,16},{24,28},{28,24},{1,5},{5... | collective-permute-start | bytes 196616 | tf_op jit(solution)/shard_map/ppermute | solution.py:391
  47.8 2.5 %collective-permute-start.19 = (f32[256,128]{1,0:T(8,128)S(1)}, f32[256,128]{1,0:T(8,128)S(1)}, u32[]{:S(2)}, u32[]{:S(2)}) collective-permute-start(f32[256,128]{1,0:T(8,128)S(1)} %max.46.near), channel_id=1, source_target_pairs={{0,1},{1,0},{2,3},{3,2},{4,5},{5,4},{6,7},{7,6},{8,9},{9,8},{10,11... | collective-permute-start | bytes 393224 | tf_op jit(solution)/shard_map/ppermute | solution.py:391
  50.4 6.0 %collective-permute-start.23 = (f32[136,128]{1,0:T(8,128)S(1)}, f32[136,128]{1,0:T(8,128)S(1)}, u32[]{:S(2)}, u32[]{:S(2)}) collective-permute-start(f32[136,128]{1,0:T(8,128)S(1)} %pad_maximum_fusion), channel_id=1, source_target_pairs={{0,16},{4,20},{8,24},{12,28},{16,0},{20,4},{24,8},{28,12},{1,17},{... | collective-permute-start | bytes 208904 | tf_op jit(solution)/shard_map/ppermute | solution.py:391
  56.5 4.7 %collective-permute-start.24 = (f32[136,128]{1,0:T(8,128)S(1)}, f32[136,128]{1,0:T(8,128)S(1)}, u32[]{:S(2)}, u32[]{:S(2)}) collective-permute-start(f32[136,128]{1,0:T(8,128)S(1)} %add_select_fusion.refs_0_), channel_id=1, source_target_pairs={{0,4},{4,0},{8,12},{12,8},{16,20},{20,16},{24,28},{28,24},{1,5},{5... | collective-permute-start | bytes 208904 | tf_op jit(solution)/shard_map/ppermute | solution.py:391
  57.7 5.8 %collective-permute-start.25 = (f32[136,128]{1,0:T(8,128)S(1)}, f32[136,128]{1,0:T(8,128)S(1)}, u32[]{:S(2)}, u32[]{:S(2)}) collective-permute-start(f32[136,128]{1,0:T(8,128)S(1)} %add_select_fusion.refs_0_), channel_id=1, source_target_pairs={{0,8},{4,12},{8,0},{12,4},{16,24},{20,28},{24,16},{28,20},{1,9},{5... | collective-permute-start | bytes 208904 | tf_op jit(solution)/shard_map/ppermute | solution.py:391
  57.7 6.1 %collective-permute-start.26 = (f32[136,128]{1,0:T(8,128)S(1)}, f32[136,128]{1,0:T(8,128)S(1)}, u32[]{:S(2)}, u32[]{:S(2)}) collective-permute-start(f32[136,128]{1,0:T(8,128)S(1)} %add_select_fusion.refs_0_), channel_id=1, source_target_pairs={{0,12},{4,8},{8,4},{12,0},{16,28},{20,24},{24,20},{28,16},{1,13},{... | collective-permute-start | bytes 208904 | tf_op jit(solution)/shard_map/ppermute | solution.py:391
  60.0 4.4 %collective-permute-start.20 = (f32[128,128]{1,0:T(8,128)S(1)}, f32[128,128]{1,0:T(8,128)S(1)}, u32[]{:S(2)}, u32[]{:S(2)}) collective-permute-start(f32[128,128]{1,0:T(8,128)S(1)} %add.48.refs_0_), channel_id=1, source_target_pairs={{0,4},{4,0},{8,12},{12,8},{16,20},{20,16},{24,28},{28,24},{1,5},{5... | collective-permute-start | bytes 196616 | tf_op jit(solution)/shard_map/ppermute | solution.py:391
  61.2 4.3 %collective-permute-start.21 = (f32[128,128]{1,0:T(8,128)S(1)}, f32[128,128]{1,0:T(8,128)S(1)}, u32[]{:S(2)}, u32[]{:S(2)}) collective-permute-start(f32[128,128]{1,0:T(8,128)S(1)} %add.48.refs_0_), channel_id=1, source_target_pairs={{0,8},{4,12},{8,0},{12,4},{16,24},{20,28},{24,16},{28,20},{1,9},{5... | collective-permute-start | bytes 196616 | tf_op jit(solution)/shard_map/ppermute | solution.py:391
  61.2 5.3 %collective-permute-start.22 = (f32[128,128]{1,0:T(8,128)S(1)}, f32[128,128]{1,0:T(8,128)S(1)}, u32[]{:S(2)}, u32[]{:S(2)}) collective-permute-start(f32[128,128]{1,0:T(8,128)S(1)} %add.48.refs_0_), channel_id=1, source_target_pairs={{0,12},{4,8},{8,4},{12,0},{16,28},{20,24},{24,20},{28,16},{1,13},{... | collective-permute-start | bytes 196616 | tf_op jit(solution)/shard_map/ppermute | solution.py:391
  66.5 1.2 collective-permute-start.27
  67.6 3.6 %collective-permute-start.28 = (f32[8,128]{1,0:T(8,128)S(1)}, f32[8,128]{1,0:T(8,128)S(1)}, u32[]{:S(2)}, u32[]{:S(2)}) collective-permute-start(f32[8,128]{1,0:T(8,128)S(1)} %add.50), channel_id=1, source_target_pairs={{0,2},{1,3},{2,0},{3,1},{4,6},{5,7},{6,4},{7,5},{8,10},{9,11},{10,... | collective-permute-start | bytes 12296 | tf_op jit(solution)/shard_map/ppermute | solution.py:391
  74.6 1.4 %collective-permute-start.29 = (f32[256,128]{1,0:T(8,128)S(1)}, f32[256,128]{1,0:T(8,128)S(1)}, u32[]{:S(2)}, u32[]{:S(2)}) collective-permute-start(f32[256,128]{1,0:T(8,128)S(1)} %get-tuple-element.101), channel_id=1, source_target_pairs={{0,1},{1,0},{2,3},{3,2},{4,5},{5,4},{6,7},{7,6},{8,9},{9,8},{10,11... | collective-permute-start | bytes 393224 | tf_op jit(solution)/shard_map/ppermute | solution.py:391
  76.0 5.6 %collective-permute-start.30 = (f32[256,128]{1,0:T(8,128)S(1)}, f32[256,128]{1,0:T(8,128)S(1)}, u32[]{:S(2)}, u32[]{:S(2)}) collective-permute-start(f32[256,128]{1,0:T(8,128)S(1)} %add.52), channel_id=1, source_target_pairs={{0,2},{1,3},{2,0},{3,1},{4,6},{5,7},{6,4},{7,5},{8,10},{9,11},{10,... | collective-permute-start | bytes 393224 | tf_op jit(solution)/shard_map/ppermute | solution.py:391
  81.6 1.4 %collective-permute-start.31 = (f32[256,128]{1,0:T(8,128)S(1)}, f32[256,128]{1,0:T(8,128)S(1)}, u32[]{:S(2)}, u32[]{:S(2)}) collective-permute-start(f32[256,128]{1,0:T(8,128)S(1)} %add.53.refs_0_), channel_id=1, source_target_pairs={{0,1},{1,0},{2,3},{3,2},{4,5},{5,4},{6,7},{7,6},{8,9},{9,8},{10,11... | collective-permute-start | bytes 393224 | tf_op jit(solution)/shard_map/ppermute | solution.py:391
  86.2 4.3 %collective-permute-start.33 = (f32[128,128]{1,0:T(8,128)S(1)}, f32[128,128]{1,0:T(8,128)S(1)}, u32[]{:S(2)}, u32[]{:S(2)}) collective-permute-start(f32[128,128]{1,0:T(8,128)S(1)} %get-tuple-element.105), channel_id=1, source_target_pairs={{0,8},{4,12},{8,0},{12,4},{16,24},{20,28},{24,16},{28,20},{1,9},{5... | collective-permute-start | bytes 196616 | tf_op jit(solution)/shard_map/ppermute | solution.py:391
  88.3 5.2 %collective-permute-start.34 = (f32[128,128]{1,0:T(8,128)S(1)}, f32[128,128]{1,0:T(8,128)S(1)}, u32[]{:S(2)}, u32[]{:S(2)}) collective-permute-start(f32[128,128]{1,0:T(8,128)S(1)} %get-tuple-element.106), channel_id=1, source_target_pairs={{0,12},{4,8},{8,4},{12,0},{16,28},{20,24},{24,20},{28,16},{1,13},{... | collective-permute-start | bytes 196616 | tf_op jit(solution)/shard_map/ppermute | solution.py:391
  89.3 4.8 %collective-permute-start.32 = (f32[128,128]{1,0:T(8,128)S(1)}, f32[128,128]{1,0:T(8,128)S(1)}, u32[]{:S(2)}, u32[]{:S(2)}) collective-permute-start(f32[128,128]{1,0:T(8,128)S(1)} %get-tuple-element.104), channel_id=1, source_target_pairs={{0,4},{4,0},{8,12},{12,8},{16,20},{20,16},{24,28},{28,24},{1,5},{5... | collective-permute-start | bytes 196616 | tf_op jit(solution)/shard_map/ppermute | solution.py:391
  94.1 5.9 %collective-permute-start.35 = (f32[128,128]{1,0:T(8,128)S(1)}, f32[128,128]{1,0:T(8,128)S(1)}, u32[]{:S(2)}, u32[]{:S(2)}) collective-permute-start(f32[128,128]{1,0:T(8,128)S(1)} %add_add_fusion), channel_id=1, source_target_pairs={{0,16},{4,20},{8,24},{12,28},{16,0},{20,4},{24,8},{28,12},{1,17},{... | collective-permute-start | bytes 196616 | tf_op jit(solution)/shard_map/ppermute | solution.py:391
  100.1 4.3 %collective-permute-start.36 = (f32[128,128]{1,0:T(8,128)S(1)}, f32[128,128]{1,0:T(8,128)S(1)}, u32[]{:S(2)}, u32[]{:S(2)}) collective-permute-start(f32[128,128]{1,0:T(8,128)S(1)} %add.57.refs_0_), channel_id=1, source_target_pairs={{0,4},{4,0},{8,12},{12,8},{16,20},{20,16},{24,28},{28,24},{1,5},{5... | collective-permute-start | bytes 196616 | tf_op jit(solution)/shard_map/ppermute | solution.py:391
  101.0 4.3 %collective-permute-start.37 = (f32[128,128]{1,0:T(8,128)S(1)}, f32[128,128]{1,0:T(8,128)S(1)}, u32[]{:S(2)}, u32[]{:S(2)}) collective-permute-start(f32[128,128]{1,0:T(8,128)S(1)} %add.57.refs_0_), channel_id=1, source_target_pairs={{0,8},{4,12},{8,0},{12,4},{16,24},{20,28},{24,16},{28,20},{1,9},{5... | collective-permute-start | bytes 196616 | tf_op jit(solution)/shard_map/ppermute | solution.py:391
  101.5 5.2 %collective-permute-start.38 = (f32[128,128]{1,0:T(8,128)S(1)}, f32[128,128]{1,0:T(8,128)S(1)}, u32[]{:S(2)}, u32[]{:S(2)}) collective-permute-start(f32[128,128]{1,0:T(8,128)S(1)} %add.57.refs_0_), channel_id=1, source_target_pairs={{0,12},{4,8},{8,4},{12,0},{16,28},{20,24},{24,20},{28,16},{1,13},{... | collective-permute-start | bytes 196616 | tf_op jit(solution)/shard_map/ppermute | solution.py:391
  110.6 1.3 %collective-permute-start.39 = (f32[256,128]{1,0:T(8,128)S(1)}, f32[256,128]{1,0:T(8,128)S(1)}, u32[]{:S(2)}, u32[]{:S(2)}) collective-permute-start(f32[256,128]{1,0:T(8,128)S(1)} %get-tuple-element.110), channel_id=1, source_target_pairs={{0,1},{1,0},{2,3},{3,2},{4,5},{5,4},{6,7},{7,6},{8,9},{9,8},{10,11... | collective-permute-start | bytes 393224 | tf_op jit(solution)/shard_map/ppermute | solution.py:391
  112.0 5.7 %collective-permute-start.40 = (f32[256,128]{1,0:T(8,128)S(1)}, f32[256,128]{1,0:T(8,128)S(1)}, u32[]{:S(2)}, u32[]{:S(2)}) collective-permute-start(f32[256,128]{1,0:T(8,128)S(1)} %add.58), channel_id=1, source_target_pairs={{0,2},{1,3},{2,0},{3,1},{4,6},{5,7},{6,4},{7,5},{8,10},{9,11},{10,... | collective-permute-start | bytes 393224 | tf_op jit(solution)/shard_map/ppermute | solution.py:391
  117.7 1.4 %collective-permute-start.41 = (f32[256,128]{1,0:T(8,128)S(1)}, f32[256,128]{1,0:T(8,128)S(1)}, u32[]{:S(2)}, u32[]{:S(2)}) collective-permute-start(f32[256,128]{1,0:T(8,128)S(1)} %add.59.refs_0_), channel_id=1, source_target_pairs={{0,1},{1,0},{2,3},{3,2},{4,5},{5,4},{6,7},{7,6},{8,9},{9,8},{10,11... | collective-permute-start | bytes 393224 | tf_op jit(solution)/shard_map/ppermute | solution.py:391
where the time goes:
time: 120 us
  starting transfers between devices  45.1 us (38%)
  waiting for transfers between devices  44.7 us (37%)
  Pallas kernels  28.1 us (23%)
    ppermute x42, starting transfers between devices, swap(): return lax.ppermute(vector, axis, [(i, i ^ bit) for i in range(size)])  45.1 us
    ppermute x42, waiting for transfers between devices, swap(): return lax.ppermute(vector, axis, [(i, i ^ bit) for i in range(size)])  44.7 us
    pallas_call x6, Pallas kernels, call_blocks(): pl.pallas_call(kernel, out_shape=out_shape, in_specs=[pl.BlockSpec(memory...  27 us
  transfers between devices with their start and end apart: 42, of which 29 were waited for; matrix products, arithmetic and copies ran while one was open for 0% of the time, Pallas kernels for 3%

commit v1 on v0

--- a/solution.py
+++ b/solution.py
@@ -11,7 +11,8 @@
 STEP_SCALE = 0.3
 
 CHUNKS = 8
-GROUP = 32
+FIRST_GROUP = 32
+GROUP = 64
 AHEAD = 3
 ROW_HALVING = 1
 QUARTERS = 4
@@ -44,9 +45,9 @@
     return pl.ds(pl.multiple_of(chunk * size, size), size)
 
 
-def piece_chunk(pieces, place, size):
+def piece_chunk(pieces, place, size, offset=0):
     per_piece = CHUNKS // len(pieces)
-    start = (place % per_piece) * size
+    start = offset + (place % per_piece) * size
     return pieces[place // per_piece], pl.ds(start, size)
 
 
@@ -75,24 +76,24 @@
 
 
 def block_copy(index, values_ref, blocks, arrived):
-    part = pl.ds(pl.multiple_of(index * GROUP, GROUP), GROUP)
+    part = pl.ds(pl.multiple_of(index * FIRST_GROUP, FIRST_GROUP), FIRST_GROUP)
     return pltpu.make_async_copy(values_ref.at[part], blocks.at[part], arrived.at[index])
 
 
-def for_slots(ids_ref, visit, finish, before=None):
+def for_slots(ids_ref, visit, finish, group=GROUP, before=None):
     count = ids_ref.shape[0] // 2
 
     def step(index, carry):
         if before is not None:
             before(index)
-        slots = [index * GROUP + inner for inner in range(GROUP)]
+        slots = [index * group + inner for inner in range(group)]
         ids = [(ids_ref[slot], ids_ref[count + slot]) for slot in slots]
         terms = visit(slots, ids)
         for (row, col), term in zip(ids, terms):
             finish(row, col, term)
         return carry
 
-    lax.fori_loop(0, count // GROUP, step, 0)
+    lax.fori_loop(0, count // group, step, 0)
 
 
 def product_terms(vector_ref, tiles, blocks):
@@ -130,7 +131,7 @@
     row_out, col_out, blocks = refs[:2], refs[2:6], refs[6]
     arrived, row_acc, col_acc = refs[7:]
     mask, across = col_mask(), row_mask()
-    groups = values_ref.shape[0] // GROUP
+    groups = values_ref.shape[0] // FIRST_GROUP
     for index in range(min(AHEAD, groups)):
         block_copy(index, values_ref, blocks, arrived).start()
     for acc in (row_acc, col_acc):
@@ -151,7 +152,7 @@
         add_row(row_acc, row_place(row, count, across), terms[0], jnp.maximum)
         add_row(col_acc, col_place(col, count, mask), terms[1], jnp.maximum)
 
-    for_slots(ids_ref, visit, finish, before)
+    for_slots(ids_ref, visit, finish, FIRST_GROUP, before)
     store_pieces(row_acc, row_out, count)
     store_pieces(col_acc, col_out, count)
 
@@ -250,7 +251,7 @@
         scaled = scale * vector_ref[part, :]
         sums.append(fold_rows(scaled * scaled))
     squares[...] = tree_sum(sums)
-    tail = pl.ds(pieces[0].shape[0] - 8, 8)
+    tail = pl.ds(count // QUARTERS, 8)
     demand_squares[...] = tree_sum([piece[tail, :] for piece in pieces])
 
 
@@ -264,14 +265,18 @@
     product, refs = refs[:4], refs[4:]
     scale_ref, cost_ref, low_ref, high_ref, kind_ref, primal_ref = refs[:6]
     cost_squares, demand_squares, primal_out = refs[6:9]
-    row_out, (shifted, row_acc) = refs[9:11], refs[11:]
+    row_out, refs = refs[9:11], refs[11:]
+    shifted, row_acc = refs[:2]
+    moved_ref = primal_out
+    if last:
+        moved_ref, written = refs[2:]
     mask, across = col_mask(), row_mask()
     size = count // CHUNKS
     row_acc[...] = jnp.zeros_like(row_acc)
     primal_step = STEP_SCALE / norm_ratio(cost_squares, demand_squares)
     for place in range(CHUNKS):
         part = chunk_rows(place ^ mask, size)
-        piece, inside = piece_chunk(product, place, size)
+        piece, inside = piece_chunk(product, place, size, product[0].shape[0] - count // QUARTERS)
         scale = scale_ref[part, :]
         inverse = 1.0 / scale
         primal = primal_ref[part, :]
@@ -287,7 +292,11 @@
             (kind == 2) | (kind == 3), jnp.minimum(moved, high_ref[part, :] * inverse), moved
         )
         shifted[part, :] = scale * (2.0 * moved - primal)
-        primal_out[part, :] = scale * moved if last else moved
+        moved_ref[part, :] = scale * moved if last else moved
+
+    if last:
+        copy_out = pltpu.make_async_copy(moved_ref, primal_out, written)
+        copy_out.start()
 
     def visit(slots, ids):
         return product_terms(shifted, [col for _, col in ids], [turned[slot] for slot in slots])
@@ -297,6 +306,8 @@
 
     for_slots(ids_ref, visit, finish)
     store_pieces(row_acc, row_out, count)
+    if last:
+        copy_out.wait()
 
 
 def next_dual(first, image, inside, scale, demand, dual, dual_step):
@@ -364,19 +375,26 @@
     )(*operands)
 
 
-def call_blocks(kernel, ids, values, operands, out_shape, scratch, first=False):
+def call_blocks(kernel, ids, values, operands, out_shape, scratch, first=False, last=False):
     width = values.shape[1]
     scratch_shapes = [pltpu.VMEM((rows, width), jnp.float32) for rows in scratch]
     if first:
-        arrivals = pltpu.SemaphoreType.DMA((values.shape[0] // GROUP,))
+        arrivals = pltpu.SemaphoreType.DMA((values.shape[0] // FIRST_GROUP,))
         scratch_shapes = [arrivals] + scratch_shapes
+    out_specs = [pl.BlockSpec(memory_space=pltpu.VMEM)] * len(out_shape)
+    if last:
+        out_specs[0] = pl.BlockSpec(memory_space=pl.ANY)
+        scratch_shapes = scratch_shapes + [
+            pltpu.VMEM(out_shape[0].shape, out_shape[0].dtype),
+            pltpu.SemaphoreType.DMA,
+        ]
     return pl.pallas_call(
         kernel,
         out_shape=out_shape,
         in_specs=[pl.BlockSpec(memory_space=pltpu.SMEM)]
         + [pl.BlockSpec(memory_space=pl.ANY if first else pltpu.VMEM)]
         + [pl.BlockSpec(memory_space=pltpu.VMEM)] * len(operands),
-        out_specs=[pl.BlockSpec(memory_space=pltpu.VMEM)] * len(out_shape),
+        out_specs=out_specs,
         scratch_shapes=scratch_shapes,
         compiler_params=pltpu.CompilerParams(
             vmem_limit_bytes=FIRST_VMEM if first else BLOCK_VMEM
@@ -434,11 +452,8 @@
 
 
 def sum_cols(vector, groups):
-    bit = 1
-    while bit < groups:
-        vector = vector + swap(vector, "col", groups, bit)
-        bit *= 2
-    return vector
+    parts = [vector] + [swap(vector, "col", groups, mask) for mask in range(1, groups)]
+    return tree_sum(parts)
 
 
 def per_device(
@@ -518,6 +533,7 @@
         [spare] * 2,
     )
     row_scale, col_scale = out[6:]
+    out, product = lax.optimization_barrier((out, product))
     near = halve_rows(out[:2], col_groups, jnp.maximum)
     share = scatter_cols(out[2:6], row_groups, jnp.maximum, (near,))
     row_peaks = join_rows(exchange_rows(near, col_groups, jnp.maximum), col_groups)
@@ -526,15 +542,15 @@
         row_peaks + [row_scale, demand],
         whole + squares,
     )
-    share = after(jnp.concatenate([share, demand_squares], axis=0), product)
-    product = gather_cols(after(product, share), row_groups)
-    gathered = gather_cols(exchange_cols(share, row_groups, mixed), row_groups)
+    share = jnp.concatenate([share, demand_squares], axis=0)
+    share = exchange_cols(share, row_groups, mixed)
+    gathered = gather_cols(jnp.concatenate([share, product], axis=0), row_groups)
     col_scale, cost_squares, demand_squares = call_plain(
         functools.partial(col_scale_kernel, count),
         gathered + [col_scale, cost_vec],
         whole + squares + squares,
     )
-    norms = [sum_cols(after(cost_squares, product), col_groups), demand_squares]
+    norms = [sum_cols(cost_squares, col_groups), demand_squares]
 
     def forward(first, last, product, primal):
         out = call_blocks(
@@ -544,10 +560,11 @@
             product + [col_scale, cost_vec, lower, upper, bound_kind, primal] + norms,
             whole + row_pieces,
             [count, spare],
+            last=last,
         )
         return out[0], over_col(out[1:], jnp.add)
 
-    primal, image = forward(True, False, product, primal_start)
+    primal, image = forward(True, False, gathered, primal_start)
     out = call_blocks(
         functools.partial(transposed_kernel, count, True),
         ids,

time: 120 us -> 115 us (0.958)
  starting transfers between devices: 45.1 us -> 39.7 us
  waiting for transfers between devices: 44.7 us -> 47.5 us
  Pallas kernels: 28.1 us -> 25.5 us
    ppermute x42 -> x40, starting transfers between devices: 45.1 us -> 39.7 us  [swap(): return lax.ppermute(vector, axis, [(i, i ^ bit) for i in range(size)])]
    ppermute x42 -> x40, waiting for transfers between devices: 44.7 us -> 47.5 us  [swap(): return lax.ppermute(vector, axis, [(i, i ^ bit) for i in range(size)])]
    pallas_call x6, Pallas kernels: 27 us -> 24.5 us  [call_blocks(): pl.pallas_call(kernel, out_shape=out_shape, in_specs=[pl.BlockSpec(memory...]
  transfers between devices with their start and end apart: 42 -> 40, of which waited for: 29 -> 26; matrix products, arithmetic and copies ran while one was open for 0% -> 0% of each run, Pallas kernels for 3% -> 9%
where the time goes in v1:
time: 115 us
  waiting for transfers between devices  47.5 us (41%)
  starting transfers between devices  39.7 us (35%)
  Pallas kernels  25.5 us (22%)
    ppermute x40, waiting for transfers between devices, swap(): return lax.ppermute(vector, axis, [(i, i ^ bit) for i in range(size)])  47.5 us
    ppermute x40, starting transfers between devices, swap(): return lax.ppermute(vector, axis, [(i, i ^ bit) for i in range(size)])  39.7 us
    pallas_call x6, Pallas kernels, call_blocks(): pl.pallas_call(kernel, out_shape=out_shape, in_specs=[pl.BlockSpec(memory...  24.5 us
  transfers between devices with their start and end apart: 40, of which 26 were waited for; matrix products, arithmetic and copies ran while one was open for 0% of the time, Pallas kernels for 9%

profile of v1, /device:TPU:0, one launch (start us, length us, event | category | flops | bytes accessed | tf_op | source)
XLA Modules:
  0.0 114.8 jit_solution(13587827609398103886)
XLA Ops:
  0.6 0.7 pad_add_fusion.ids_ref
  1.4 5.7 %shard_map.113 = (f32[256,128]{1,0:T(8,128)S(1)}, f32[256,128]{1,0:T(8,128)S(1)}, f32[128,128]{1,0:T(8,128)S(1)}, f32[128,128]{1,0:T(8,128)S(1)}, f32[128,128]{1...) custom-call(s32[512]{0:T(512)S(1)} %pad_add_fusion.ids_ref, bf16[256,128,128]{2,1,0:T(8,128)(2,1)} %bitcast.27), custom_call_target="tpu_custom_call" | custom-call | flops 8388608 | bytes 8388608 | tf_op jit(solution)/shard_map/pallas_call | solution.py:391
  7.1 0.6 collective-permute-start
  7.6 3.5 %collective-permute-start.5 = (f32[128,128]{1,0:T(8,128)S(1)}, f32[128,128]{1,0:T(8,128)S(1)}, u32[]{:S(2)}, u32[]{:S(2)}) collective-permute-start(f32[128,128]{1,0:T(8,128)S(1)} %get-tuple-element.71), channel_id=1, source_target_pairs={{0,12},{4,8},{8,4},{12,0},{16,28},{20,24},{24,20},{28,16},{1,13},{... | collective-permute-start | bytes 196616 | tf_op jit(solution)/shard_map/ppermute | solution.py:409
  11.2 0.4 collective-permute-start.4
  11.6 1.5 %collective-permute-start.3 = (f32[128,128]{1,0:T(8,128)S(1)}, f32[128,128]{1,0:T(8,128)S(1)}, u32[]{:S(2)}, u32[]{:S(2)}) collective-permute-start(f32[128,128]{1,0:T(8,128)S(1)} %get-tuple-element.69), channel_id=1, source_target_pairs={{0,4},{4,0},{8,12},{12,8},{16,20},{20,16},{24,28},{28,24},{1,5},{5... | collective-permute-start | bytes 196616 | tf_op jit(solution)/shard_map/ppermute | solution.py:409
  13.1 1.6 %collective-permute-start.1 = (f32[256,128]{1,0:T(8,128)S(1)}, f32[256,128]{1,0:T(8,128)S(1)}, u32[]{:S(2)}, u32[]{:S(2)}) collective-permute-start(f32[256,128]{1,0:T(8,128)S(1)} %max.36), channel_id=1, source_target_pairs={{0,2},{1,3},{2,0},{3,1},{4,6},{5,7},{6,4},{7,5},{8,10},{9,11},{10,... | collective-permute-start | bytes 393224 | tf_op jit(solution)/shard_map/ppermute | solution.py:409
  14.7 3.1 %shard_map.114 = (f32[128,128]{1,0:T(8,128)S(1)}, f32[128,128]{1,0:T(8,128)S(1)}, f32[128,128]{1,0:T(8,128)S(1)}, f32[128,128]{1,0:T(8,128)S(1)}, bf16[256,128,128]{2,1,0:T(8,128)(2,1)S(1)}) custom-call(s32[512]{0:T(512)S(1)} %pad_add_fusion.ids_ref, bf16[256,128,128]{2,1,0:T(8,128)(2,1)S(1)} %get-tuple-element.61.blocks, f32[512,128]{1,0:T(8,128)S(1)} %bitcast.18), custom_call_target="tpu_custom_call" | custom-call | flops 8388608 | bytes 8388608 | tf_op jit(solution)/shard_map/pallas_call | solution.py:391
  17.9 2.6 %collective-permute-start.6 = (f32[128,128]{1,0:T(8,128)S(1)}, f32[128,128]{1,0:T(8,128)S(1)}, u32[]{:S(2)}, u32[]{:S(2)}) collective-permute-start(f32[128,128]{1,0:T(8,128)S(1)} %maximum_maximum_fusion.1), channel_id=1, source_target_pairs={{0,16},{4,20},{8,24},{12,28},{16,0},{20,4},{24,8},{28,12},{1,17},{... | collective-permute-start | bytes 196616 | tf_op jit(solution)/shard_map/ppermute | solution.py:409
  20.5 0.8 collective-permute-start.11
  21.3 1.3 %collective-permute-start.12 = (f32[128,128]{1,0:T(8,128)S(1)}, f32[128,128]{1,0:T(8,128)S(1)}, u32[]{:S(2)}, u32[]{:S(2)}) collective-permute-start(f32[128,128]{1,0:T(8,128)S(1)} %get-tuple-element.80), channel_id=1, source_target_pairs={{0,12},{4,8},{8,4},{12,0},{16,28},{20,24},{24,20},{28,16},{1,13},{... | collective-permute-start | bytes 196616 | tf_op jit(solution)/shard_map/ppermute | solution.py:409
  22.6 1.5 %collective-permute-start.10 = (f32[128,128]{1,0:T(8,128)S(1)}, f32[128,128]{1,0:T(8,128)S(1)}, u32[]{:S(2)}, u32[]{:S(2)}) collective-permute-start(f32[128,128]{1,0:T(8,128)S(1)} %get-tuple-element.78), channel_id=1, source_target_pairs={{0,4},{4,0},{8,12},{12,8},{16,20},{20,16},{24,28},{28,24},{1,5},{5... | collective-permute-start | bytes 196616 | tf_op jit(solution)/shard_map/ppermute | solution.py:409
  24.1 0.6 collective-permute-start.7
  24.7 0.5 collective-permute-done.11
  25.2 1.0 collective-permute-start.8
  26.2 0.2 collective-permute-done.12
  26.5 1.3 %collective-permute-start.9 = (f32[128,128]{1,0:T(8,128)S(1)}, f32[128,128]{1,0:T(8,128)S(1)}, u32[]{:S(2)}, u32[]{:S(2)}) collective-permute-start(f32[128,128]{1,0:T(8,128)S(1)} %max.41.refs_2_), channel_id=1, source_target_pairs={{0,12},{4,8},{8,4},{12,0},{16,28},{20,24},{24,20},{28,16},{1,13},{... | collective-permute-start | bytes 196616 | tf_op jit(solution)/shard_map/ppermute | solution.py:409
  27.8 2.2 %collective-permute-start.13 = (f32[128,128]{1,0:T(8,128)S(1)}, f32[128,128]{1,0:T(8,128)S(1)}, u32[]{:S(2)}, u32[]{:S(2)}) collective-permute-start(f32[128,128]{1,0:T(8,128)S(1)} %add_add_fusion.1), channel_id=1, source_target_pairs={{0,16},{4,20},{8,24},{12,28},{16,0},{20,4},{24,8},{28,12},{1,17},{... | collective-permute-start | bytes 196616 | tf_op jit(solution)/shard_map/ppermute | solution.py:409
  30.1 2.2 %collective-permute-done.9.refs_5_ = f32[128,128]{1,0:T(8,128)S(1)} collective-permute-done((f32[128,128]{1,0:T(8,128)S(1)}, f32[128,128]{1,0:T(8,128)S(1)}, u32[]{:S(2)}, u32[]{:S(2)}) %collective-permute-start.9) | collective-permute-done | bytes 65568 | tf_op jit(solution)/shard_map/ppermute | solution.py:409
  32.3 7.0 %shard_map.115 = (f32[256,128]{1,0:T(8,128)S(1)}, f32[256,128]{1,0:T(8,128)S(1)}, f32[128,128]{1,0:T(8,128)S(1)}, f32[128,128]{1,0:T(8,128)S(1)}, f32[128,128]{1...) custom-call(s32[512]{0:T(512)S(1)} %pad_add_fusion.ids_ref, ...), custom_call_target="tpu_custom_call" | custom-call | flops 8388608 | bytes 8388608 | tf_op jit(solution)/shard_map/pallas_call | solution.py:391
  39.4 1.3 %collective-permute-done.14 = f32[256,128]{1,0:T(8,128)S(1)} collective-permute-done((f32[256,128]{1,0:T(8,128)S(1)}, f32[256,128]{1,0:T(8,128)S(1)}, u32[]{:S(2)}, u32[]{:S(2)}) %collective-permute-start.14) | collective-permute-done | bytes 131104 | tf_op jit(solution)/shard_map/ppermute | solution.py:409
  40.8 0.5 collective-permute-start.18
  41.3 1.3 %collective-permute-start.17 = (f32[128,128]{1,0:T(8,128)S(1)}, f32[128,128]{1,0:T(8,128)S(1)}, u32[]{:S(2)}, u32[]{:S(2)}) collective-permute-start(f32[128,128]{1,0:T(8,128)S(1)} %get-tuple-element.102), channel_id=1, source_target_pairs={{0,12},{4,8},{8,4},{12,0},{16,28},{20,24},{24,20},{28,16},{1,13},{... | collective-permute-start | bytes 196616 | tf_op jit(solution)/shard_map/ppermute | solution.py:409
  42.6 1.4 %collective-permute-start.16 = (f32[128,128]{1,0:T(8,128)S(1)}, f32[128,128]{1,0:T(8,128)S(1)}, u32[]{:S(2)}, u32[]{:S(2)}) collective-permute-start(f32[128,128]{1,0:T(8,128)S(1)} %get-tuple-element.101), channel_id=1, source_target_pairs={{0,8},{4,12},{8,0},{12,4},{16,24},{20,28},{24,16},{28,20},{1,9},{5... | collective-permute-start | bytes 196616 | tf_op jit(solution)/shard_map/ppermute | solution.py:409
  44.1 0.7 collective-permute-start.15
  44.8 1.6 %collective-permute-done.18 = f32[256,128]{1,0:T(8,128)S(1)} collective-permute-done((f32[256,128]{1,0:T(8,128)S(1)}, f32[256,128]{1,0:T(8,128)S(1)}, u32[]{:S(2)}, u32[]{:S(2)}) %collective-permute-start.18) | collective-permute-done | bytes 131104 | tf_op jit(solution)/shard_map/ppermute | solution.py:409
  46.5 0.4 collective-permute-done.17
  46.9 0.4 collective-permute-done.16
  47.3 1.0 collective-permute-done.15
  48.5 1.1 collective-permute-start.20
  49.5 5.1 %collective-permute-done.20 = f32[136,128]{1,0:T(8,128)S(1)} collective-permute-done((f32[136,128]{1,0:T(8,128)S(1)}, f32[136,128]{1,0:T(8,128)S(1)}, u32[]{:S(2)}, u32[]{:S(2)}) %collective-permute-start.20) | collective-permute-done | bytes 69664 | tf_op jit(solution)/shard_map/ppermute | solution.py:409
  54.7 1.3 %collective-permute-start.21 = (f32[264,128]{1,0:T(8,128)S(1)}, f32[264,128]{1,0:T(8,128)S(1)}, u32[]{:S(2)}, u32[]{:S(2)}) collective-permute-start(f32[264,128]{1,0:T(8,128)S(1)} %pad_maximum_fusion.refs_0_), channel_id=1, source_target_pairs={{0,4},{4,0},{8,12},{12,8},{16,20},{20,16},{24,28},{28,24},{1,5},{5... | collective-permute-start | bytes 405512 | tf_op jit(solution)/shard_map/ppermute | solution.py:409
  56.0 2.3 %collective-permute-start.23 = (f32[264,128]{1,0:T(8,128)S(1)}, f32[264,128]{1,0:T(8,128)S(1)}, u32[]{:S(2)}, u32[]{:S(2)}) collective-permute-start(f32[264,128]{1,0:T(8,128)S(1)} %pad_maximum_fusion.refs_0_), channel_id=1, source_target_pairs={{0,12},{4,8},{8,4},{12,0},{16,28},{20,24},{24,20},{28,16},{1,13},{... | collective-permute-start | bytes 405512 | tf_op jit(solution)/shard_map/ppermute | solution.py:409
  58.3 2.1 %collective-permute-done.21.refs_1_ = f32[264,128]{1,0:T(8,128)S(1)} collective-permute-done((f32[264,128]{1,0:T(8,128)S(1)}, f32[264,128]{1,0:T(8,128)S(1)}, u32[]{:S(2)}, u32[]{:S(2)}) %collective-permute-start.21) | collective-permute-done | bytes 135200 | tf_op jit(solution)/shard_map/ppermute | solution.py:409
  60.4 2.1 %collective-permute-done.22.refs_2_ = f32[264,128]{1,0:T(8,128)S(1)} collective-permute-done((f32[264,128]{1,0:T(8,128)S(1)}, f32[264,128]{1,0:T(8,128)S(1)}, u32[]{:S(2)}, u32[]{:S(2)}) %collective-permute-start.22) | collective-permute-done | bytes 135200 | tf_op jit(solution)/shard_map/ppermute | solution.py:409
  62.5 1.4 %collective-permute-done.23.refs_3_ = f32[264,128]{1,0:T(8,128)S(1)} collective-permute-done((f32[264,128]{1,0:T(8,128)S(1)}, f32[264,128]{1,0:T(8,128)S(1)}, u32[]{:S(2)}, u32[]{:S(2)}) %collective-permute-start.23) | collective-permute-done | bytes 135200 | tf_op jit(solution)/shard_map/ppermute | solution.py:409
  64.0 0.3 collective-permute-start.25
  64.2 1.9 %collective-permute-start.24 = (f32[8,128]{1,0:T(8,128)S(1)}, f32[8,128]{1,0:T(8,128)S(1)}, u32[]{:S(2)}, u32[]{:S(2)}) collective-permute-start(f32[8,128]{1,0:T(8,128)S(1)} %get-tuple-element.106), channel_id=1, source_target_pairs={{0,1},{1,0},{2,3},{3,2},{4,5},{5,4},{6,7},{7,6},{8,9},{9,8},{10,11... | collective-permute-start | bytes 12296 | tf_op jit(solution)/shard_map/ppermute | solution.py:409
  66.2 1.5 %collective-permute-done.25 = f32[8,128]{1,0:T(8,128)S(1)} collective-permute-done((f32[8,128]{1,0:T(8,128)S(1)}, f32[8,128]{1,0:T(8,128)S(1)}, u32[]{:S(2)}, u32[]{:S(2)}) %collective-permute-start.25) | collective-permute-done | bytes 4128 | tf_op jit(solution)/shard_map/ppermute | solution.py:409
  67.7 2.9 %shard_map.118 = (f32[512,128]{1,0:T(8,128)S(1)}, f32[256,128]{1,0:T(8,128)S(1)}, f32[256,128]{1,0:T(8,128)S(1)}) custom-call(s32[512]{0:T(512)S(1)} %pad_add_fusion.ids_ref, bf16[256,128,128]{2,1,0:T(8,128)(2,1)S(1)} %get-tuple-element.65.turned, f32[264,128]{1,0:T(8,128)S(1)} %pad_maximum_fusion.refs_0_, f32[264,128]{1,0:T(8,128)S(1)} %collective-permute-done.21.refs_1_, ...), custom_call_target="tpu_custom_call" | custom-call | flops 8388608 | bytes 8388608 | tf_op jit(solution)/shard_map/pallas_call | solution.py:391
  70.6 0.2 collective-permute-start.27
  70.8 1.2 %collective-permute-done.27 = f32[256,128]{1,0:T(8,128)S(1)} collective-permute-done((f32[256,128]{1,0:T(8,128)S(1)}, f32[256,128]{1,0:T(8,128)S(1)}, u32[]{:S(2)}, u32[]{:S(2)}) %collective-permute-start.27) | collective-permute-done | bytes 131104 | tf_op jit(solution)/shard_map/ppermute | solution.py:409
  72.0 1.4 %collective-permute-start.28 = (f32[256,128]{1,0:T(8,128)S(1)}, f32[256,128]{1,0:T(8,128)S(1)}, u32[]{:S(2)}, u32[]{:S(2)}) collective-permute-start(f32[256,128]{1,0:T(8,128)S(1)} %add.56), channel_id=1, source_target_pairs={{0,2},{1,3},{2,0},{3,1},{4,6},{5,7},{6,4},{7,5},{8,10},{9,11},{10,... | collective-permute-start | bytes 393224 | tf_op jit(solution)/shard_map/ppermute | solution.py:409
  73.4 4.2 %collective-permute-done.28 = f32[256,128]{1,0:T(8,128)S(1)} collective-permute-done((f32[256,128]{1,0:T(8,128)S(1)}, f32[256,128]{1,0:T(8,128)S(1)}, u32[]{:S(2)}, u32[]{:S(2)}) %collective-permute-start.28) | collective-permute-done | bytes 131104 | tf_op jit(solution)/shard_map/ppermute | solution.py:409
  77.8 1.3 %collective-permute-done.29.refs_1_ = f32[256,128]{1,0:T(8,128)S(1)} collective-permute-done((f32[256,128]{1,0:T(8,128)S(1)}, f32[256,128]{1,0:T(8,128)S(1)}, u32[]{:S(2)}, u32[]{:S(2)}) %collective-permute-start.29) | collective-permute-done | bytes 131104 | tf_op jit(solution)/shard_map/ppermute | solution.py:409
  79.1 2.8 %shard_map.119 = (f32[512,128]{1,0:T(8,128)S(1)}, f32[128,128]{1,0:T(8,128)S(1)}, f32[128,128]{1,0:T(8,128)S(1)}, f32[128,128]{1,0:T(8,128)S(1)}, f32[128,128]{1,0:T(8,128)S(1)}) custom-call(s32[512]{0:T(512)S(1)} %pad_add_fusion.ids_ref, bf16[256,128,128]{2,1,0:T(8,128)(2,1)S(1)} %get-tuple-element.61.blocks, f32[256,128]{1,0:T(8,128)S(1)} %add.57.refs_0_, ...), custom_call_target="tpu_custom_call" | custom-call | flops 8388608 | bytes 8388608 | tf_op jit(solution)/shard_map/pallas_call | solution.py:391
  81.9 0.2 collective-permute-start.31
  82.1 2.8 %collective-permute-start.32 = (f32[128,128]{1,0:T(8,128)S(1)}, f32[128,128]{1,0:T(8,128)S(1)}, u32[]{:S(2)}, u32[]{:S(2)}) collective-permute-start(f32[128,128]{1,0:T(8,128)S(1)} %get-tuple-element.114), channel_id=1, source_target_pairs={{0,12},{4,8},{8,4},{12,0},{16,28},{20,24},{24,20},{28,16},{1,13},{... | collective-permute-start | bytes 196616 | tf_op jit(solution)/shard_map/ppermute | solution.py:409
  84.9 0.6 collective-permute-start.30
  85.5 1.1 collective-permute-done.31
  86.6 2.2 %collective-permute-done.32 = f32[128,128]{1,0:T(8,128)S(1)} collective-permute-done((f32[128,128]{1,0:T(8,128)S(1)}, f32[128,128]{1,0:T(8,128)S(1)}, u32[]{:S(2)}, u32[]{:S(2)}) %collective-permute-start.32) | collective-permute-done | bytes 65568 | tf_op jit(solution)/shard_map/ppermute | solution.py:409
  88.8 1.1 collective-permute-done.30
  90.0 6.0 %collective-permute-done.33 = f32[128,128]{1,0:T(8,128)S(1)} collective-permute-done((f32[128,128]{1,0:T(8,128)S(1)}, f32[128,128]{1,0:T(8,128)S(1)}, u32[]{:S(2)}, u32[]{:S(2)}) %collective-permute-start.33) | collective-permute-done | bytes 65568 | tf_op jit(solution)/shard_map/ppermute | solution.py:409
  96.0 0.3 collective-permute-start.34
  96.3 0.3 collective-permute-start.35
  96.6 2.9 %collective-permute-start.36 = (f32[128,128]{1,0:T(8,128)S(1)}, f32[128,128]{1,0:T(8,128)S(1)}, u32[]{:S(2)}, u32[]{:S(2)}) collective-permute-start(f32[128,128]{1,0:T(8,128)S(1)} %add.61.refs_0_), channel_id=1, source_target_pairs={{0,12},{4,8},{8,4},{12,0},{16,28},{20,24},{24,20},{28,16},{1,13},{... | collective-permute-start | bytes 196616 | tf_op jit(solution)/shard_map/ppermute | solution.py:409
  99.6 1.5 %collective-permute-done.34.refs_1_ = f32[128,128]{1,0:T(8,128)S(1)} collective-permute-done((f32[128,128]{1,0:T(8,128)S(1)}, f32[128,128]{1,0:T(8,128)S(1)}, u32[]{:S(2)}, u32[]{:S(2)}) %collective-permute-start.34) | collective-permute-done | bytes 65568 | tf_op jit(solution)/shard_map/ppermute | solution.py:409
  101.0 1.5 %collective-permute-done.36.refs_3_ = f32[128,128]{1,0:T(8,128)S(1)} collective-permute-done((f32[128,128]{1,0:T(8,128)S(1)}, f32[128,128]{1,0:T(8,128)S(1)}, u32[]{:S(2)}, u32[]{:S(2)}) %collective-permute-start.36) | collective-permute-done | bytes 65568 | tf_op jit(solution)/shard_map/ppermute | solution.py:409
  102.5 2.9 %shard_map.120 = (f32[512,128]{1,0:T(8,128)}, f32[256,128]{1,0:T(8,128)S(1)}, f32[256,128]{1,0:T(8,128)S(1)}) custom-call(s32[512]{0:T(512)S(1)} %pad_add_fusion.ids_ref, bf16[256,128,128]{2,1,0:T(8,128)(2,1)S(1)} %get-tuple-element.65.turned, f32[128,128]{1,0:T(8,128)S(1)} %add.61.refs_0_, f32[128,128]{1,0:T(8,128)S(1)} %collective-permute-done.34.refs_1_, ...), custom_call_target="tpu_custom_call" | custom-call | flops 8388608 | bytes 8388608 | tf_op jit(solution)/shard_map/pallas_call | solution.py:391
  105.5 1.3 %collective-permute-done.37 = f32[256,128]{1,0:T(8,128)S(1)} collective-permute-done((f32[256,128]{1,0:T(8,128)S(1)}, f32[256,128]{1,0:T(8,128)S(1)}, u32[]{:S(2)}, u32[]{:S(2)}) %collective-permute-start.37) | collective-permute-done | bytes 131104 | tf_op jit(solution)/shard_map/ppermute | solution.py:409
  106.9 0.9 collective-permute-start.38
  107.8 4.7 %collective-permute-done.38 = f32[256,128]{1,0:T(8,128)S(1)} collective-permute-done((f32[256,128]{1,0:T(8,128)S(1)}, f32[256,128]{1,0:T(8,128)S(1)}, u32[]{:S(2)}, u32[]{:S(2)}) %collective-permute-start.38) | collective-permute-done | bytes 131104 | tf_op jit(solution)/shard_map/ppermute | solution.py:409
  112.6 1.3 %collective-permute-done.39.refs_1_ = f32[256,128]{1,0:T(8,128)S(1)} collective-permute-done((f32[256,128]{1,0:T(8,128)S(1)}, f32[256,128]{1,0:T(8,128)S(1)}, u32[]{:S(2)}, u32[]{:S(2)}) %collective-permute-start.39) | collective-permute-done | bytes 131104 | tf_op jit(solution)/shard_map/ppermute | solution.py:409
  113.9 0.9 shard_map.121
  (60 shorter events, 1.1 us)
Async XLA Ops:
  0.6 14.0 %copy-start.2 = (f32[65536]{0:T(1024)S(1)}, f32[65536]{0:T(1024)}, u32[]{:S(2)}) copy-start(f32[65536]{0:T(1024)} %param.19) | copy-start | bytes 786436
  7.1 4.1 %collective-permute-start = (f32[256,128]{1,0:T(8,128)S(1)}, f32[256,128]{1,0:T(8,128)S(1)}, u32[]{:S(2)}, u32[]{:S(2)}) collective-permute-start(f32[256,128]{1,0:T(8,128)S(1)} %get-tuple-element.63), channel_id=1, source_target_pairs={{0,1},{1,0},{2,3},{3,2},{4,5},{5,4},{6,7},{7,6},{8,9},{9,8},{10,11... | collective-permute-start | bytes 393224 | tf_op jit(solution)/shard_map/ppermute | solution.py:409
  7.6 10.2 %collective-permute-start.5 = (f32[128,128]{1,0:T(8,128)S(1)}, f32[128,128]{1,0:T(8,128)S(1)}, u32[]{:S(2)}, u32[]{:S(2)}) collective-permute-start(f32[128,128]{1,0:T(8,128)S(1)} %get-tuple-element.71), channel_id=1, source_target_pairs={{0,12},{4,8},{8,4},{12,0},{16,28},{20,24},{24,20},{28,16},{1,13},{... | collective-permute-start | bytes 196616 | tf_op jit(solution)/shard_map/ppermute | solution.py:409
  11.2 6.7 %collective-permute-start.4 = (f32[128,128]{1,0:T(8,128)S(1)}, f32[128,128]{1,0:T(8,128)S(1)}, u32[]{:S(2)}, u32[]{:S(2)}) collective-permute-start(f32[128,128]{1,0:T(8,128)S(1)} %get-tuple-element.70), channel_id=1, source_target_pairs={{0,8},{4,12},{8,0},{12,4},{16,24},{20,28},{24,16},{28,20},{1,9},{5... | collective-permute-start | bytes 196616 | tf_op jit(solution)/shard_map/ppermute | solution.py:409
  11.6 6.3 %collective-permute-start.3 = (f32[128,128]{1,0:T(8,128)S(1)}, f32[128,128]{1,0:T(8,128)S(1)}, u32[]{:S(2)}, u32[]{:S(2)}) collective-permute-start(f32[128,128]{1,0:T(8,128)S(1)} %get-tuple-element.69), channel_id=1, source_target_pairs={{0,4},{4,0},{8,12},{12,8},{16,20},{20,16},{24,28},{28,24},{1,5},{5... | collective-permute-start | bytes 196616 | tf_op jit(solution)/shard_map/ppermute | solution.py:409
  13.1 7.4 %collective-permute-start.1 = (f32[256,128]{1,0:T(8,128)S(1)}, f32[256,128]{1,0:T(8,128)S(1)}, u32[]{:S(2)}, u32[]{:S(2)}) collective-permute-start(f32[256,128]{1,0:T(8,128)S(1)} %max.36), channel_id=1, source_target_pairs={{0,2},{1,3},{2,0},{3,1},{4,6},{5,7},{6,4},{7,5},{8,10},{9,11},{10,... | collective-permute-start | bytes 393224 | tf_op jit(solution)/shard_map/ppermute | solution.py:409
  14.7 33.7 %copy-start = (f32[65536]{0:T(1024)S(1)}, f32[65536]{0:T(1024)}, u32[]{:S(2)}) copy-start(f32[65536]{0:T(1024)} %param.14) | copy-start | bytes 786436
  17.8 46.1 %copy-start.1 = (f32[65536]{0:T(1024)S(1)}, f32[65536]{0:T(1024)}, u32[]{:S(2)}) copy-start(f32[65536]{0:T(1024)} %param.13) | copy-start | bytes 786436
  17.8 49.8 %copy-start.3 = (f32[65536]{0:T(1024)S(1)}, f32[65536]{0:T(1024)}, u32[]{:S(2)}) copy-start(f32[65536]{0:T(1024)} %param.15) | copy-start | bytes 786436
  17.8 49.8 %copy-start.4 = (f32[65536]{0:T(1024)S(1)}, f32[65536]{0:T(1024)}, u32[]{:S(2)}) copy-start(f32[65536]{0:T(1024)} %param.16) | copy-start | bytes 786436
  17.8 49.8 %copy-start.5 = (s32[65536]{0:T(1024)S(1)}, s32[65536]{0:T(1024)}, u32[]{:S(2)}) copy-start(s32[65536]{0:T(1024)} %param.17) | copy-start | bytes 786436
  17.9 49.8 %copy-start.6 = (f32[65536]{0:T(1024)S(1)}, f32[65536]{0:T(1024)}, u32[]{:S(2)}) copy-start(f32[65536]{0:T(1024)} %param.18) | copy-start | bytes 786436
  17.9 6.1 %collective-permute-start.6 = (f32[128,128]{1,0:T(8,128)S(1)}, f32[128,128]{1,0:T(8,128)S(1)}, u32[]{:S(2)}, u32[]{:S(2)}) collective-permute-start(f32[128,128]{1,0:T(8,128)S(1)} %maximum_maximum_fusion.1), channel_id=1, source_target_pairs={{0,16},{4,20},{8,24},{12,28},{16,0},{20,4},{24,8},{28,12},{1,17},{... | collective-permute-start | bytes 196616 | tf_op jit(solution)/shard_map/ppermute | solution.py:409
  20.5 4.7 %collective-permute-start.11 = (f32[128,128]{1,0:T(8,128)S(1)}, f32[128,128]{1,0:T(8,128)S(1)}, u32[]{:S(2)}, u32[]{:S(2)}) collective-permute-start(f32[128,128]{1,0:T(8,128)S(1)} %get-tuple-element.79), channel_id=1, source_target_pairs={{0,8},{4,12},{8,0},{12,4},{16,24},{20,28},{24,16},{28,20},{1,9},{5... | collective-permute-start | bytes 196616 | tf_op jit(solution)/shard_map/ppermute | solution.py:409
  21.3 5.2 %collective-permute-start.12 = (f32[128,128]{1,0:T(8,128)S(1)}, f32[128,128]{1,0:T(8,128)S(1)}, u32[]{:S(2)}, u32[]{:S(2)}) collective-permute-start(f32[128,128]{1,0:T(8,128)S(1)} %get-tuple-element.80), channel_id=1, source_target_pairs={{0,12},{4,8},{8,4},{12,0},{16,28},{20,24},{24,20},{28,16},{1,13},{... | collective-permute-start | bytes 196616 | tf_op jit(solution)/shard_map/ppermute | solution.py:409
  22.6 5.2 %collective-permute-start.10 = (f32[128,128]{1,0:T(8,128)S(1)}, f32[128,128]{1,0:T(8,128)S(1)}, u32[]{:S(2)}, u32[]{:S(2)}) collective-permute-start(f32[128,128]{1,0:T(8,128)S(1)} %get-tuple-element.78), channel_id=1, source_target_pairs={{0,4},{4,0},{8,12},{12,8},{16,20},{20,16},{24,28},{28,24},{1,5},{5... | collective-permute-start | bytes 196616 | tf_op jit(solution)/shard_map/ppermute | solution.py:409
  24.1 8.2 %collective-permute-start.2 = (f32[256,128]{1,0:T(8,128)S(1)}, f32[256,128]{1,0:T(8,128)S(1)}, u32[]{:S(2)}, u32[]{:S(2)}) collective-permute-start(f32[256,128]{1,0:T(8,128)S(1)} %max.37.refs_0_), channel_id=1, source_target_pairs={{0,1},{1,0},{2,3},{3,2},{4,5},{5,4},{6,7},{7,6},{8,9},{9,8},{10,11... | collective-permute-start | bytes 393224 | tf_op jit(solution)/shard_map/ppermute | solution.py:409
  24.1 5.9 %collective-permute-start.7 = (f32[128,128]{1,0:T(8,128)S(1)}, f32[128,128]{1,0:T(8,128)S(1)}, u32[]{:S(2)}, u32[]{:S(2)}) collective-permute-start(f32[128,128]{1,0:T(8,128)S(1)} %max.41.refs_2_), channel_id=1, source_target_pairs={{0,4},{4,0},{8,12},{12,8},{16,20},{20,16},{24,28},{28,24},{1,5},{5... | collective-permute-start | bytes 196616 | tf_op jit(solution)/shard_map/ppermute | solution.py:409
  25.2 4.9 %collective-permute-start.8 = (f32[128,128]{1,0:T(8,128)S(1)}, f32[128,128]{1,0:T(8,128)S(1)}, u32[]{:S(2)}, u32[]{:S(2)}) collective-permute-start(f32[128,128]{1,0:T(8,128)S(1)} %max.41.refs_2_), channel_id=1, source_target_pairs={{0,8},{4,12},{8,0},{12,4},{16,24},{20,28},{24,16},{28,20},{1,9},{5... | collective-permute-start | bytes 196616 | tf_op jit(solution)/shard_map/ppermute | solution.py:409
  26.5 5.8 %collective-permute-start.9 = (f32[128,128]{1,0:T(8,128)S(1)}, f32[128,128]{1,0:T(8,128)S(1)}, u32[]{:S(2)}, u32[]{:S(2)}) collective-permute-start(f32[128,128]{1,0:T(8,128)S(1)} %max.41.refs_2_), channel_id=1, source_target_pairs={{0,12},{4,8},{8,4},{12,0},{16,28},{20,24},{24,20},{28,16},{1,13},{... | collective-permute-start | bytes 196616 | tf_op jit(solution)/shard_map/ppermute | solution.py:409
  27.8 11.6 %collective-permute-start.13 = (f32[128,128]{1,0:T(8,128)S(1)}, f32[128,128]{1,0:T(8,128)S(1)}, u32[]{:S(2)}, u32[]{:S(2)}) collective-permute-start(f32[128,128]{1,0:T(8,128)S(1)} %add_add_fusion.1), channel_id=1, source_target_pairs={{0,16},{4,20},{8,24},{12,28},{16,0},{20,4},{24,8},{28,12},{1,17},{... | collective-permute-start | bytes 196616 | tf_op jit(solution)/shard_map/ppermute | solution.py:409
  39.3 1.4 %collective-permute-start.14 = (f32[256,128]{1,0:T(8,128)S(1)}, f32[256,128]{1,0:T(8,128)S(1)}, u32[]{:S(2)}, u32[]{:S(2)}) collective-permute-start(f32[256,128]{1,0:T(8,128)S(1)} %get-tuple-element.99), channel_id=1, source_target_pairs={{0,1},{1,0},{2,3},{3,2},{4,5},{5,4},{6,7},{7,6},{8,9},{9,8},{10,11... | collective-permute-start | bytes 393224 | tf_op jit(solution)/shard_map/ppermute | solution.py:409
  40.8 5.6 %collective-permute-start.18 = (f32[256,128]{1,0:T(8,128)S(1)}, f32[256,128]{1,0:T(8,128)S(1)}, u32[]{:S(2)}, u32[]{:S(2)}) collective-permute-start(f32[256,128]{1,0:T(8,128)S(1)} %max.42), channel_id=1, source_target_pairs={{0,2},{1,3},{2,0},{3,1},{4,6},{5,7},{6,4},{7,5},{8,10},{9,11},{10,... | collective-permute-start | bytes 393224 | tf_op jit(solution)/shard_map/ppermute | solution.py:409
  41.3 5.6 %collective-permute-start.17 = (f32[128,128]{1,0:T(8,128)S(1)}, f32[128,128]{1,0:T(8,128)S(1)}, u32[]{:S(2)}, u32[]{:S(2)}) collective-permute-start(f32[128,128]{1,0:T(8,128)S(1)} %get-tuple-element.102), channel_id=1, source_target_pairs={{0,12},{4,8},{8,4},{12,0},{16,28},{20,24},{24,20},{28,16},{1,13},{... | collective-permute-start | bytes 196616 | tf_op jit(solution)/shard_map/ppermute | solution.py:409
  42.6 4.7 %collective-permute-start.16 = (f32[128,128]{1,0:T(8,128)S(1)}, f32[128,128]{1,0:T(8,128)S(1)}, u32[]{:S(2)}, u32[]{:S(2)}) collective-permute-start(f32[128,128]{1,0:T(8,128)S(1)} %get-tuple-element.101), channel_id=1, source_target_pairs={{0,8},{4,12},{8,0},{12,4},{16,24},{20,28},{24,16},{28,20},{1,9},{5... | collective-permute-start | bytes 196616 | tf_op jit(solution)/shard_map/ppermute | solution.py:409
  44.1 4.3 %collective-permute-start.15 = (f32[128,128]{1,0:T(8,128)S(1)}, f32[128,128]{1,0:T(8,128)S(1)}, u32[]{:S(2)}, u32[]{:S(2)}) collective-permute-start(f32[128,128]{1,0:T(8,128)S(1)} %get-tuple-element.100), channel_id=1, source_target_pairs={{0,4},{4,0},{8,12},{12,8},{16,20},{20,16},{24,28},{28,24},{1,5},{5... | collective-permute-start | bytes 196616 | tf_op jit(solution)/shard_map/ppermute | solution.py:409
  46.4 1.9 %collective-permute-start.19 = (f32[256,128]{1,0:T(8,128)S(1)}, f32[256,128]{1,0:T(8,128)S(1)}, u32[]{:S(2)}, u32[]{:S(2)}) collective-permute-start(f32[256,128]{1,0:T(8,128)S(1)} %max.46.near), channel_id=1, source_target_pairs={{0,1},{1,0},{2,3},{3,2},{4,5},{5,4},{6,7},{7,6},{8,9},{9,8},{10,11... | collective-permute-start | bytes 393224 | tf_op jit(solution)/shard_map/ppermute | solution.py:409
  48.5 6.2 %collective-permute-start.20 = (f32[136,128]{1,0:T(8,128)S(1)}, f32[136,128]{1,0:T(8,128)S(1)}, u32[]{:S(2)}, u32[]{:S(2)}) collective-permute-start(f32[136,128]{1,0:T(8,128)S(1)} %pad_maximum_fusion.1), channel_id=1, source_target_pairs={{0,16},{4,20},{8,24},{12,28},{16,0},{20,4},{24,8},{28,12},{1,17},{... | collective-permute-start | bytes 208904 | tf_op jit(solution)/shard_map/ppermute | solution.py:409
  54.7 5.7 %collective-permute-start.21 = (f32[264,128]{1,0:T(8,128)S(1)}, f32[264,128]{1,0:T(8,128)S(1)}, u32[]{:S(2)}, u32[]{:S(2)}) collective-permute-start(f32[264,128]{1,0:T(8,128)S(1)} %pad_maximum_fusion.refs_0_), channel_id=1, source_target_pairs={{0,4},{4,0},{8,12},{12,8},{16,20},{20,16},{24,28},{28,24},{1,5},{5... | collective-permute-start | bytes 405512 | tf_op jit(solution)/shard_map/ppermute | solution.py:409
  56.0 6.5 %collective-permute-start.22 = (f32[264,128]{1,0:T(8,128)S(1)}, f32[264,128]{1,0:T(8,128)S(1)}, u32[]{:S(2)}, u32[]{:S(2)}) collective-permute-start(f32[264,128]{1,0:T(8,128)S(1)} %pad_maximum_fusion.refs_0_), channel_id=1, source_target_pairs={{0,8},{4,12},{8,0},{12,4},{16,24},{20,28},{24,16},{28,20},{1,9},{5... | collective-permute-start | bytes 405512 | tf_op jit(solution)/shard_map/ppermute | solution.py:409
  56.0 7.9 %collective-permute-start.23 = (f32[264,128]{1,0:T(8,128)S(1)}, f32[264,128]{1,0:T(8,128)S(1)}, u32[]{:S(2)}, u32[]{:S(2)}) collective-permute-start(f32[264,128]{1,0:T(8,128)S(1)} %pad_maximum_fusion.refs_0_), channel_id=1, source_target_pairs={{0,12},{4,8},{8,4},{12,0},{16,28},{20,24},{24,20},{28,16},{1,13},{... | collective-permute-start | bytes 405512 | tf_op jit(solution)/shard_map/ppermute | solution.py:409
  64.0 3.7 %collective-permute-start.25 = (f32[8,128]{1,0:T(8,128)S(1)}, f32[8,128]{1,0:T(8,128)S(1)}, u32[]{:S(2)}, u32[]{:S(2)}) collective-permute-start(f32[8,128]{1,0:T(8,128)S(1)} %get-tuple-element.106), channel_id=1, source_target_pairs={{0,2},{1,3},{2,0},{3,1},{4,6},{5,7},{6,4},{7,5},{8,10},{9,11},{10,... | collective-permute-start | bytes 12296 | tf_op jit(solution)/shard_map/ppermute | solution.py:409
  64.2 3.4 %collective-permute-start.26 = (f32[8,128]{1,0:T(8,128)S(1)}, f32[8,128]{1,0:T(8,128)S(1)}, u32[]{:S(2)}, u32[]{:S(2)}) collective-permute-start(f32[8,128]{1,0:T(8,128)S(1)} %get-tuple-element.106), channel_id=1, source_target_pairs={{0,3},{1,2},{2,1},{3,0},{4,7},{5,6},{6,5},{7,4},{8,11},{9,10},{10,... | collective-permute-start | bytes 12296 | tf_op jit(solution)/shard_map/ppermute | solution.py:409
  64.2 3.4 %collective-permute-start.24 = (f32[8,128]{1,0:T(8,128)S(1)}, f32[8,128]{1,0:T(8,128)S(1)}, u32[]{:S(2)}, u32[]{:S(2)}) collective-permute-start(f32[8,128]{1,0:T(8,128)S(1)} %get-tuple-element.106), channel_id=1, source_target_pairs={{0,1},{1,0},{2,3},{3,2},{4,5},{5,4},{6,7},{7,6},{8,9},{9,8},{10,11... | collective-permute-start | bytes 12296 | tf_op jit(solution)/shard_map/ppermute | solution.py:409
  70.6 1.4 %collective-permute-start.27 = (f32[256,128]{1,0:T(8,128)S(1)}, f32[256,128]{1,0:T(8,128)S(1)}, u32[]{:S(2)}, u32[]{:S(2)}) collective-permute-start(f32[256,128]{1,0:T(8,128)S(1)} %get-tuple-element.109), channel_id=1, source_target_pairs={{0,1},{1,0},{2,3},{3,2},{4,5},{5,4},{6,7},{7,6},{8,9},{9,8},{10,11... | collective-permute-start | bytes 393224 | tf_op jit(solution)/shard_map/ppermute | solution.py:409
  72.0 5.6 %collective-permute-start.28 = (f32[256,128]{1,0:T(8,128)S(1)}, f32[256,128]{1,0:T(8,128)S(1)}, u32[]{:S(2)}, u32[]{:S(2)}) collective-permute-start(f32[256,128]{1,0:T(8,128)S(1)} %add.56), channel_id=1, source_target_pairs={{0,2},{1,3},{2,0},{3,1},{4,6},{5,7},{6,4},{7,5},{8,10},{9,11},{10,... | collective-permute-start | bytes 393224 | tf_op jit(solution)/shard_map/ppermute | solution.py:409
  77.7 1.4 %collective-permute-start.29 = (f32[256,128]{1,0:T(8,128)S(1)}, f32[256,128]{1,0:T(8,128)S(1)}, u32[]{:S(2)}, u32[]{:S(2)}) collective-permute-start(f32[256,128]{1,0:T(8,128)S(1)} %add.57.refs_0_), channel_id=1, source_target_pairs={{0,1},{1,0},{2,3},{3,2},{4,5},{5,4},{6,7},{7,6},{8,9},{9,8},{10,11... | collective-permute-start | bytes 393224 | tf_op jit(solution)/shard_map/ppermute | solution.py:409
  81.9 4.7 %collective-permute-start.31 = (f32[128,128]{1,0:T(8,128)S(1)}, f32[128,128]{1,0:T(8,128)S(1)}, u32[]{:S(2)}, u32[]{:S(2)}) collective-permute-start(f32[128,128]{1,0:T(8,128)S(1)} %get-tuple-element.113), channel_id=1, source_target_pairs={{0,8},{4,12},{8,0},{12,4},{16,24},{20,28},{24,16},{28,20},{1,9},{5... | collective-permute-start | bytes 196616 | tf_op jit(solution)/shard_map/ppermute | solution.py:409
  82.1 6.7 %collective-permute-start.32 = (f32[128,128]{1,0:T(8,128)S(1)}, f32[128,128]{1,0:T(8,128)S(1)}, u32[]{:S(2)}, u32[]{:S(2)}) collective-permute-start(f32[128,128]{1,0:T(8,128)S(1)} %get-tuple-element.114), channel_id=1, source_target_pairs={{0,12},{4,8},{8,4},{12,0},{16,28},{20,24},{24,20},{28,16},{1,13},{... | collective-permute-start | bytes 196616 | tf_op jit(solution)/shard_map/ppermute | solution.py:409
  84.9 5.0 %collective-permute-start.30 = (f32[128,128]{1,0:T(8,128)S(1)}, f32[128,128]{1,0:T(8,128)S(1)}, u32[]{:S(2)}, u32[]{:S(2)}) collective-permute-start(f32[128,128]{1,0:T(8,128)S(1)} %get-tuple-element.112), channel_id=1, source_target_pairs={{0,4},{4,0},{8,12},{12,8},{16,20},{20,16},{24,28},{28,24},{1,5},{5... | collective-permute-start | bytes 196616 | tf_op jit(solution)/shard_map/ppermute | solution.py:409
  89.9 6.1 %collective-permute-start.33 = (f32[128,128]{1,0:T(8,128)S(1)}, f32[128,128]{1,0:T(8,128)S(1)}, u32[]{:S(2)}, u32[]{:S(2)}) collective-permute-start(f32[128,128]{1,0:T(8,128)S(1)} %add_add_fusion), channel_id=1, source_target_pairs={{0,16},{4,20},{8,24},{12,28},{16,0},{20,4},{24,8},{28,12},{1,17},{... | collective-permute-start | bytes 196616 | tf_op jit(solution)/shard_map/ppermute | solution.py:409
  96.0 5.0 %collective-permute-start.34 = (f32[128,128]{1,0:T(8,128)S(1)}, f32[128,128]{1,0:T(8,128)S(1)}, u32[]{:S(2)}, u32[]{:S(2)}) collective-permute-start(f32[128,128]{1,0:T(8,128)S(1)} %add.61.refs_0_), channel_id=1, source_target_pairs={{0,4},{4,0},{8,12},{12,8},{16,20},{20,16},{24,28},{28,24},{1,5},{5... | collective-permute-start | bytes 196616 | tf_op jit(solution)/shard_map/ppermute | solution.py:409
  96.3 4.7 %collective-permute-start.35 = (f32[128,128]{1,0:T(8,128)S(1)}, f32[128,128]{1,0:T(8,128)S(1)}, u32[]{:S(2)}, u32[]{:S(2)}) collective-permute-start(f32[128,128]{1,0:T(8,128)S(1)} %add.61.refs_0_), channel_id=1, source_target_pairs={{0,8},{4,12},{8,0},{12,4},{16,24},{20,28},{24,16},{28,20},{1,9},{5... | collective-permute-start | bytes 196616 | tf_op jit(solution)/shard_map/ppermute | solution.py:409
  96.6 5.9 %collective-permute-start.36 = (f32[128,128]{1,0:T(8,128)S(1)}, f32[128,128]{1,0:T(8,128)S(1)}, u32[]{:S(2)}, u32[]{:S(2)}) collective-permute-start(f32[128,128]{1,0:T(8,128)S(1)} %add.61.refs_0_), channel_id=1, source_target_pairs={{0,12},{4,8},{8,4},{12,0},{16,28},{20,24},{24,20},{28,16},{1,13},{... | collective-permute-start | bytes 196616 | tf_op jit(solution)/shard_map/ppermute | solution.py:409
  105.4 1.4 %collective-permute-start.37 = (f32[256,128]{1,0:T(8,128)S(1)}, f32[256,128]{1,0:T(8,128)S(1)}, u32[]{:S(2)}, u32[]{:S(2)}) collective-permute-start(f32[256,128]{1,0:T(8,128)S(1)} %get-tuple-element.118), channel_id=1, source_target_pairs={{0,1},{1,0},{2,3},{3,2},{4,5},{5,4},{6,7},{7,6},{8,9},{9,8},{10,11... | collective-permute-start | bytes 393224 | tf_op jit(solution)/shard_map/ppermute | solution.py:409
  106.9 5.6 %collective-permute-start.38 = (f32[256,128]{1,0:T(8,128)S(1)}, f32[256,128]{1,0:T(8,128)S(1)}, u32[]{:S(2)}, u32[]{:S(2)}) collective-permute-start(f32[256,128]{1,0:T(8,128)S(1)} %add.62), channel_id=1, source_target_pairs={{0,2},{1,3},{2,0},{3,1},{4,6},{5,7},{6,4},{7,5},{8,10},{9,11},{10,... | collective-permute-start | bytes 393224 | tf_op jit(solution)/shard_map/ppermute | solution.py:409
  112.5 1.4 %collective-permute-start.39 = (f32[256,128]{1,0:T(8,128)S(1)}, f32[256,128]{1,0:T(8,128)S(1)}, u32[]{:S(2)}, u32[]{:S(2)}) collective-permute-start(f32[256,128]{1,0:T(8,128)S(1)} %add.63.refs_0_), channel_id=1, source_target_pairs={{0,1},{1,0},{2,3},{3,2},{4,5},{5,4},{6,7},{7,6},{8,9},{9,8},{10,11... | collective-permute-start | bytes 393224 | tf_op jit(solution)/shard_map/ppermute | solution.py:409

commit v2 on v1

--- a/solution.py
+++ b/solution.py
@@ -175,18 +175,16 @@
     store_pieces(product_acc, product_out, count)
 
 
-def second_pass_kernel(count, ids_ref, blocks, *refs):
-    row_in, col_in, row_out, col_out = refs[:2], refs[2:6], refs[6:8], refs[8:12]
-    row_scale, col_scale, row_acc, col_acc = refs[12:]
+def second_cols_kernel(count, ids_ref, blocks, *refs):
+    row_in, product_in, col_out, row_scale, col_acc = (
+        refs[:2], refs[2:6], refs[6:10], refs[10], refs[11]
+    )
     mask, across = col_mask(), row_mask()
     size = count // CHUNKS
-    row_acc[...] = jnp.zeros_like(row_acc)
     col_acc[...] = jnp.zeros_like(col_acc)
     for place in range(CHUNKS):
         piece, part = piece_chunk(row_in, place, size)
         row_scale[chunk_rows(place ^ across, size), :] = lax.rsqrt(piece[part, :] + SMALL_EPS)
-        piece, part = piece_chunk(col_in, place, size)
-        col_scale[chunk_rows(place ^ mask, size), :] = lax.rsqrt(piece[part, :] + SMALL_EPS)
     width = blocks.shape[-1]
     square = (width, width)
     diagonal = lax.broadcasted_iota(jnp.int32, square, 0) == lax.broadcasted_iota(
@@ -194,9 +192,8 @@
     )
     diagonal = diagonal.astype(jnp.float32).astype(jnp.bfloat16)
 
-    def peaks(row, col, slot):
+    def peaks(row, slot):
         sizes = jnp.abs(blocks[slot])
-        by_col = sizes.astype(jnp.float32) * one_row(col_scale, col)
         scale = one_row(row_scale, row)
         high = scale.astype(jnp.bfloat16)
         low = (scale - high.astype(jnp.float32)).astype(jnp.bfloat16)
@@ -205,22 +202,46 @@
             jnp.concatenate([sizes, sizes], axis=0),
             preferred_element_type=jnp.float32,
         )
-        return row_max(by_col.T), row_max(by_row)
+        return row_max(by_row)
 
     def visit(slots, ids):
-        return [peaks(row, col, slot) for slot, (row, col) in zip(slots, ids)]
-
-    def finish(row, col, terms):
-        add_row(row_acc, row_place(row, count, across), terms[0], jnp.maximum)
-        add_row(col_acc, col_place(col, count, mask), terms[1], jnp.maximum)
+        return [peaks(row, slot) for slot, (row, _) in zip(slots, ids)]
+
+    def finish(row, col, term):
+        add_row(col_acc, col_place(col, count, mask), term, jnp.maximum)
 
     for_slots(ids_ref, visit, finish)
+    quarter = count // QUARTERS
+    for index, (piece, product) in enumerate(zip(col_out, product_in)):
+        piece[pl.ds(0, quarter), :] = col_acc[pl.ds(index * quarter, quarter), :]
+        piece[pl.ds(quarter, quarter), :] = product[...]
+
+
+def second_rows_kernel(count, ids_ref, blocks, *refs):
+    col_in, row_out, col_scale, row_acc = refs[:4], refs[4:6], refs[6], refs[7]
+    mask, across = col_mask(), row_mask()
+    size = count // CHUNKS
+    row_acc[...] = jnp.zeros_like(row_acc)
     for place in range(CHUNKS):
-        part = pl.ds(place * size, size)
-        piece, inside = piece_chunk(row_out, place, size)
-        piece[inside, :] = row_acc[part, :] * row_scale[chunk_rows(place ^ across, size), :]
-        piece, inside = piece_chunk(col_out, place, size)
-        piece[inside, :] = col_acc[part, :] * col_scale[chunk_rows(place ^ mask, size), :]
+        piece, part = piece_chunk(col_in, place, size)
+        col_scale[chunk_rows(place ^ mask, size), :] = lax.rsqrt(piece[part, :] + SMALL_EPS)
+
+    def peaks(col, slot):
+        by_col = jnp.abs(blocks[slot]).astype(jnp.float32) * one_row(col_scale, col)
+        return row_max(by_col.T)
+
+    def visit(slots, ids):
+        return [peaks(col, slot) for slot, (_, col) in zip(slots, ids)]
+
+    def finish(row, col, term):
+        add_row(row_acc, row_place(row, count, across), term, jnp.maximum)
+
+    for_slots(ids_ref, visit, finish)
+    store_pieces(row_acc, row_out, count)
+
+
+def next_scale(scale, piece, inside):
+    return scale * lax.rsqrt(scale * piece[inside, :] + SMALL_EPS)
 
 
 def row_scale_kernel(count, near, far, scale_ref, vector_ref, new_scale, squares):
@@ -230,7 +251,7 @@
     for place in range(CHUNKS):
         part = chunk_rows(place ^ across, size)
         piece, inside = piece_chunk((near, far), place, size)
-        scale = scale_ref[part, :] * lax.rsqrt(piece[inside, :] + SMALL_EPS)
+        scale = next_scale(scale_ref[part, :], piece, inside)
         new_scale[part, :] = scale
         scaled = scale * vector_ref[part, :]
         sums.append(fold_rows(scaled * scaled))
@@ -239,20 +260,18 @@
 
 
 def col_scale_kernel(count, *refs):
-    pieces, (scale_ref, vector_ref, new_scale, squares, demand_squares) = refs[:4], refs[4:]
+    pieces, (scale_ref, vector_ref, new_scale, squares) = refs[:4], refs[4:]
     mask = col_mask()
     size = count // CHUNKS
     sums = []
     for place in range(CHUNKS):
         part = chunk_rows(place ^ mask, size)
         piece, inside = piece_chunk(pieces, place, size)
-        scale = scale_ref[part, :] * lax.rsqrt(piece[inside, :] + SMALL_EPS)
+        scale = next_scale(scale_ref[part, :], piece, inside)
         new_scale[part, :] = scale
         scaled = scale * vector_ref[part, :]
         sums.append(fold_rows(scaled * scaled))
     squares[...] = tree_sum(sums)
-    tail = pl.ds(count // QUARTERS, 8)
-    demand_squares[...] = tree_sum([piece[tail, :] for piece in pieces])
 
 
 def norm_ratio(cost_squares, demand_squares):
@@ -451,6 +470,11 @@
     return [piece, swap(piece, "row", groups, 1), swap(piece, "row", groups, 2), diagonal]
 
 
+def sum_rows(vector, groups):
+    vector = exchange_cols(vector, groups, jnp.add)
+    return tree_sum([vector] + [swap(vector, "row", groups, mask) for mask in (1, 2, 3)])
+
+
 def sum_cols(vector, groups):
     parts = [vector] + [swap(vector, "col", groups, mask) for mask in range(1, groups)]
     return tree_sum(parts)
@@ -492,7 +516,7 @@
         share = scatter_cols(pieces, row_groups, combine)
         return gather_cols(exchange_cols(share, row_groups, combine), row_groups)
 
-    tile = lax.broadcasted_iota(jnp.int32, (quarter + 8, width), 0)
+    tile = lax.broadcasted_iota(jnp.int32, (2 * quarter, width), 0)
 
     def mixed(a, b):
         return jnp.where(tile < quarter, jnp.maximum(a, b), a + b)
@@ -509,46 +533,48 @@
     )
     blocks = out[6]
     near = halve_rows(out[:2], col_groups, jnp.maximum)
+    share = scatter_cols(out[2:6], row_groups, jnp.maximum, (near,))
+    row_peaks = join_rows(exchange_rows(near, col_groups, jnp.maximum), col_groups)
     *product_pieces, turned = call_blocks(
         functools.partial(first_product_kernel, count),
         ids,
         blocks,
-        [after(dual_start, near)],
+        [after(dual_start, share)],
         col_pieces + [block_shape],
         [spare],
     )
-    share = scatter_cols(out[2:6], row_groups, jnp.maximum, (near,))
-    near = exchange_rows(near, col_groups, jnp.maximum)
-    row_peaks = join_rows(near, col_groups)
-    product = scatter_cols(after(product_pieces, near), row_groups, jnp.add)
     share = after(exchange_cols(share, row_groups, jnp.maximum), product_pieces)
-    row_peaks, col_peaks = after((row_peaks, gather_cols(share, row_groups)), product)
-    product = exchange_cols(product, row_groups, jnp.add)
-    out = call_blocks(
-        functools.partial(second_pass_kernel, count),
+    *col_pieces_2, row_scale = call_blocks(
+        functools.partial(second_cols_kernel, count),
         ids,
         blocks,
-        row_peaks + col_peaks,
-        row_pieces + col_pieces + whole + whole,
-        [spare] * 2,
-    )
-    row_scale, col_scale = out[6:]
-    out, product = lax.optimization_barrier((out, product))
-    near = halve_rows(out[:2], col_groups, jnp.maximum)
-    share = scatter_cols(out[2:6], row_groups, jnp.maximum, (near,))
-    row_peaks = join_rows(exchange_rows(near, col_groups, jnp.maximum), col_groups)
+        after(row_peaks, share) + product_pieces,
+        vectors(*[2 * quarter] * QUARTERS) + whole,
+        [spare],
+    )
+    col_peaks = gather_cols(share, row_groups)
+    share = scatter_cols(after(col_pieces_2, col_peaks), row_groups, mixed)
+    near, far, col_scale = call_blocks(
+        functools.partial(second_rows_kernel, count),
+        ids,
+        blocks,
+        col_peaks,
+        row_pieces + whole,
+        [spare],
+    )
+    near, far = after((near, far), share)
+    share = exchange_cols(share, row_groups, mixed)
     row_scale, demand_squares = call_plain(
         functools.partial(row_scale_kernel, count),
-        row_peaks + [row_scale, demand],
+        over_col([near, far], jnp.maximum) + [row_scale, demand],
         whole + squares,
     )
-    share = jnp.concatenate([share, demand_squares], axis=0)
-    share = exchange_cols(share, row_groups, mixed)
-    gathered = gather_cols(jnp.concatenate([share, product], axis=0), row_groups)
-    col_scale, cost_squares, demand_squares = call_plain(
+    demand_squares = sum_rows(demand_squares, row_groups)
+    gathered = gather_cols(share, row_groups)
+    col_scale, cost_squares = call_plain(
         functools.partial(col_scale_kernel, count),
         gathered + [col_scale, cost_vec],
-        whole + squares + squares,
+        whole + squares,
     )
     norms = [sum_cols(cost_squares, col_groups), demand_squares]
 

time: 115 us -> 117 us (1.017)
  Pallas kernels: 25.5 us -> 29.8 us
  waiting for transfers between devices: 47.5 us -> 45.6 us
    pallas_call x6 -> x7, Pallas kernels: 24.5 us -> 28.8 us  [call_blocks(): pl.pallas_call(kernel, out_shape=out_shape, in_specs=[pl.BlockSpec(memory...]
    ppermute x40, waiting for transfers between devices: 47.5 us -> 45.6 us  [swap(): return lax.ppermute(vector, axis, [(i, i ^ bit) for i in range(size)])]
  transfers between devices with their start and end apart: 40 -> 40, of which waited for: 26 -> 25; matrix products, arithmetic and copies ran while one was open for 0% -> 0% of each run, Pallas kernels for 9% -> 12%
where the time goes in v2:
time: 117 us
  waiting for transfers between devices  45.6 us (39%)
  starting transfers between devices  39.6 us (34%)
  Pallas kernels  29.8 us (25%)
    ppermute x40, waiting for transfers between devices, swap(): return lax.ppermute(vector, axis, [(i, i ^ bit) for i in range(size)])  45.6 us
    ppermute x40, starting transfers between devices, swap(): return lax.ppermute(vector, axis, [(i, i ^ bit) for i in range(size)])  39.6 us
    pallas_call x7, Pallas kernels, call_blocks(): pl.pallas_call(kernel, out_shape=out_shape, in_specs=[pl.BlockSpec(memory...  28.8 us
  transfers between devices with their start and end apart: 40, of which 25 were waited for; matrix products, arithmetic and copies ran while one was open for 0% of the time, Pallas kernels for 12%

profile of v2, /device:TPU:0, one launch (start us, length us, event | category | flops | bytes accessed | tf_op | source)
XLA Modules:
  0.0 117.3 jit_solution(4312514452225174739)
XLA Ops:
  0.6 0.7 pad_add_fusion.ids_ref
  1.4 5.7 %shard_map.113 = (f32[256,128]{1,0:T(8,128)S(1)}, f32[256,128]{1,0:T(8,128)S(1)}, f32[128,128]{1,0:T(8,128)S(1)}, f32[128,128]{1,0:T(8,128)S(1)}, f32[128,128]{1...) custom-call(s32[512]{0:T(512)S(1)} %pad_add_fusion.ids_ref, bf16[256,128,128]{2,1,0:T(8,128)(2,1)} %bitcast.27), custom_call_target="tpu_custom_call" | custom-call | flops 8388608 | bytes 8388608 | tf_op jit(solution)/shard_map/pallas_call | solution.py:410
  7.1 0.5 collective-permute-start
  7.6 1.0 collective-permute-done
  8.6 2.9 %collective-permute-start.4 = (f32[256,128]{1,0:T(8,128)S(1)}, f32[256,128]{1,0:T(8,128)S(1)}, u32[]{:S(2)}, u32[]{:S(2)}) collective-permute-start(f32[256,128]{1,0:T(8,128)S(1)} %max.36), channel_id=1, source_target_pairs={{0,2},{1,3},{2,0},{3,1},{4,6},{5,7},{6,4},{7,5},{8,10},{9,11},{10,... | collective-permute-start | bytes 393224 | tf_op jit(solution)/shard_map/ppermute | solution.py:428
  11.5 2.5 %collective-permute-start.3 = (f32[128,128]{1,0:T(8,128)S(1)}, f32[128,128]{1,0:T(8,128)S(1)}, u32[]{:S(2)}, u32[]{:S(2)}) collective-permute-start(f32[128,128]{1,0:T(8,128)S(1)} %get-tuple-element.57), channel_id=1, source_target_pairs={{0,12},{4,8},{8,4},{12,0},{16,28},{20,24},{24,20},{28,16},{1,13},{... | collective-permute-start | bytes 196616 | tf_op jit(solution)/shard_map/ppermute | solution.py:428
  14.0 0.6 collective-permute-start.1
  14.6 0.4 collective-permute-start.2
  15.0 0.3 collective-permute-done.4
  15.4 1.3 %collective-permute-done.3 = f32[128,128]{1,0:T(8,128)S(1)} collective-permute-done((f32[128,128]{1,0:T(8,128)S(1)}, f32[128,128]{1,0:T(8,128)S(1)}, u32[]{:S(2)}, u32[]{:S(2)}) %collective-permute-start.3) | collective-permute-done | bytes 65568 | tf_op jit(solution)/shard_map/ppermute | solution.py:428
  16.7 1.5 %collective-permute-done.1 = f32[128,128]{1,0:T(8,128)S(1)} collective-permute-done((f32[128,128]{1,0:T(8,128)S(1)}, f32[128,128]{1,0:T(8,128)S(1)}, u32[]{:S(2)}, u32[]{:S(2)}) %collective-permute-start.1) | collective-permute-done | bytes 65568 | tf_op jit(solution)/shard_map/ppermute | solution.py:428
  18.3 0.6 collective-permute-done.2
  18.8 2.6 %collective-permute-start.6 = (f32[128,128]{1,0:T(8,128)S(1)}, f32[128,128]{1,0:T(8,128)S(1)}, u32[]{:S(2)}, u32[]{:S(2)}) collective-permute-start(f32[128,128]{1,0:T(8,128)S(1)} %maximum_maximum_fusion), channel_id=1, source_target_pairs={{0,16},{4,20},{8,24},{12,28},{16,0},{20,4},{24,8},{28,12},{1,17},{... | collective-permute-start | bytes 196616 | tf_op jit(solution)/shard_map/ppermute | solution.py:428
  21.4 3.2 %shard_map.114 = (f32[128,128]{1,0:T(8,128)S(1)}, f32[128,128]{1,0:T(8,128)S(1)}, f32[128,128]{1,0:T(8,128)S(1)}, f32[128,128]{1,0:T(8,128)S(1)}, bf16[256,128,128]{2,1,0:T(8,128)(2,1)S(1)}) custom-call(s32[512]{0:T(512)S(1)} %pad_add_fusion.ids_ref, bf16[256,128,128]{2,1,0:T(8,128)(2,1)S(1)} %get-tuple-element.49.blocks, f32[512,128]{1,0:T(8,128)S(1)} %bitcast.18), custom_call_target="tpu_custom_call" | custom-call | flops 8388608 | bytes 8388608 | tf_op jit(solution)/shard_map/pallas_call | solution.py:410
  24.7 1.6 %collective-permute-start.9 = (f32[128,128]{1,0:T(8,128)S(1)}, f32[128,128]{1,0:T(8,128)S(1)}, u32[]{:S(2)}, u32[]{:S(2)}) collective-permute-start(f32[128,128]{1,0:T(8,128)S(1)} %max.41.refs_0_), channel_id=1, source_target_pairs={{0,12},{4,8},{8,4},{12,0},{16,28},{20,24},{24,20},{28,16},{1,13},{... | collective-permute-start | bytes 196616 | tf_op jit(solution)/shard_map/ppermute | solution.py:428
  26.3 1.5 %collective-permute-start.8 = (f32[128,128]{1,0:T(8,128)S(1)}, f32[128,128]{1,0:T(8,128)S(1)}, u32[]{:S(2)}, u32[]{:S(2)}) collective-permute-start(f32[128,128]{1,0:T(8,128)S(1)} %max.41.refs_0_), channel_id=1, source_target_pairs={{0,8},{4,12},{8,0},{12,4},{16,24},{20,28},{24,16},{28,20},{1,9},{5... | collective-permute-start | bytes 196616 | tf_op jit(solution)/shard_map/ppermute | solution.py:428
  27.8 0.5 collective-permute-start.7
  28.3 5.8 %shard_map.115 = (f32[256,128]{1,0:T(8,128)S(1)}, f32[256,128]{1,0:T(8,128)S(1)}, f32[256,128]{1,0:T(8,128)S(1)}, f32[256,128]{1,0:T(8,128)S(1)}, f32[512,128]{1,0:T(8,128)S(1)}) custom-call(s32[512]{0:T(512)S(1)} %pad_add_fusion.ids_ref, bf16[256,128,128]{2,1,0:T(8,128)(2,1)S(1)} %get-tuple-element.49.blocks, f32[256,128]{1,0:T(8,128)S(1)} %max.40.refs_0_, ...), custom_call_target="tpu_custom_call" | custom-call | flops 8388608 | bytes 8388608 | tf_op jit(solution)/shard_map/pallas_call | solution.py:410
  34.1 1.6 %collective-permute-start.10 = (f32[256,128]{1,0:T(8,128)S(1)}, f32[256,128]{1,0:T(8,128)S(1)}, u32[]{:S(2)}, u32[]{:S(2)}) collective-permute-start(f32[256,128]{1,0:T(8,128)S(1)} %get-tuple-element.72), channel_id=1, source_target_pairs={{0,4},{4,0},{8,12},{12,8},{16,20},{20,16},{24,28},{28,24},{1,5},{5... | collective-permute-start | bytes 393224 | tf_op jit(solution)/shard_map/ppermute | solution.py:428
  35.7 0.6 collective-permute-start.11
  36.2 1.4 %collective-permute-start.12 = (f32[256,128]{1,0:T(8,128)S(1)}, f32[256,128]{1,0:T(8,128)S(1)}, u32[]{:S(2)}, u32[]{:S(2)}) collective-permute-start(f32[256,128]{1,0:T(8,128)S(1)} %get-tuple-element.74), channel_id=1, source_target_pairs={{0,12},{4,8},{8,4},{12,0},{16,28},{20,24},{24,20},{28,16},{1,13},{... | collective-permute-start | bytes 393224 | tf_op jit(solution)/shard_map/ppermute | solution.py:428
  37.7 5.4 %shard_map.116 = (f32[256,128]{1,0:T(8,128)S(1)}, f32[256,128]{1,0:T(8,128)S(1)}, f32[512,128]{1,0:T(8,128)S(1)}) custom-call(s32[512]{0:T(512)S(1)} %pad_add_fusion.ids_ref, bf16[256,128,128]{2,1,0:T(8,128)(2,1)S(1)} %get-tuple-element.49.blocks, f32[128,128]{1,0:T(8,128)S(1)} %max.41.refs_0_, f32[128,128]{1,0:T(8,128)S(1)} %collective-permute-done.7.refs_1_, ...), custom_call_target="tpu_custom_call" | custom-call | flops 8388608 | bytes 8388608 | tf_op jit(solution)/shard_map/pallas_call | solution.py:410
  43.3 1.3 %collective-permute-done.20 = f32[256,128]{1,0:T(8,128)S(1)} collective-permute-done((f32[256,128]{1,0:T(8,128)S(1)}, f32[256,128]{1,0:T(8,128)S(1)}, u32[]{:S(2)}, u32[]{:S(2)}) %collective-permute-start.20) | collective-permute-done | bytes 131104 | tf_op jit(solution)/shard_map/ppermute | solution.py:428
  44.6 0.6 collective-permute-start.21
  45.2 1.8 %collective-permute-start.13 = (f32[256,128]{1,0:T(8,128)S(1)}, f32[256,128]{1,0:T(8,128)S(1)}, u32[]{:S(2)}, u32[]{:S(2)}) collective-permute-start(f32[256,128]{1,0:T(8,128)S(1)} %add_select_fusion.1), channel_id=1, source_target_pairs={{0,16},{4,20},{8,24},{12,28},{16,0},{20,4},{24,8},{28,12},{1,17},{... | collective-permute-start | bytes 393224 | tf_op jit(solution)/shard_map/ppermute | solution.py:428
  47.0 3.2 %collective-permute-done.21 = f32[256,128]{1,0:T(8,128)S(1)} collective-permute-done((f32[256,128]{1,0:T(8,128)S(1)}, f32[256,128]{1,0:T(8,128)S(1)}, u32[]{:S(2)}, u32[]{:S(2)}) %collective-permute-start.21) | collective-permute-done | bytes 131104 | tf_op jit(solution)/shard_map/ppermute | solution.py:428
  50.3 3.8 %collective-permute-done.13 = f32[256,128]{1,0:T(8,128)S(1)} collective-permute-done((f32[256,128]{1,0:T(8,128)S(1)}, f32[256,128]{1,0:T(8,128)S(1)}, u32[]{:S(2)}, u32[]{:S(2)}) %collective-permute-start.13) | collective-permute-done | bytes 131104 | tf_op jit(solution)/shard_map/ppermute | solution.py:428
  54.3 2.9 %collective-permute-start.15 = (f32[256,128]{1,0:T(8,128)S(1)}, f32[256,128]{1,0:T(8,128)S(1)}, u32[]{:S(2)}, u32[]{:S(2)}) collective-permute-start(f32[256,128]{1,0:T(8,128)S(1)} %add_select_fusion.refs_0_), channel_id=1, source_target_pairs={{0,8},{4,12},{8,0},{12,4},{16,24},{20,28},{24,16},{28,20},{1,9},{5... | collective-permute-start | bytes 393224 | tf_op jit(solution)/shard_map/ppermute | solution.py:428
  57.2 0.6 collective-permute-start.14
  57.9 0.6 collective-permute-start.23
  58.5 3.1 %collective-permute-done.16.refs_3_ = f32[256,128]{1,0:T(8,128)S(1)} collective-permute-done((f32[256,128]{1,0:T(8,128)S(1)}, f32[256,128]{1,0:T(8,128)S(1)}, u32[]{:S(2)}, u32[]{:S(2)}) %collective-permute-start.16) | collective-permute-done | bytes 131104 | tf_op jit(solution)/shard_map/ppermute | solution.py:428
  61.6 1.9 %collective-permute-done.15.refs_2_ = f32[256,128]{1,0:T(8,128)S(1)} collective-permute-done((f32[256,128]{1,0:T(8,128)S(1)}, f32[256,128]{1,0:T(8,128)S(1)}, u32[]{:S(2)}, u32[]{:S(2)}) %collective-permute-start.15) | collective-permute-done | bytes 131104 | tf_op jit(solution)/shard_map/ppermute | solution.py:428
  63.6 0.6 collective-permute-start.19
  64.1 1.1 collective-permute-start.18
  65.2 0.2 collective-permute-start.17
  65.5 0.2 collective-permute-start.26
  65.7 2.6 %collective-permute-start.25 = (f32[8,128]{1,0:T(8,128)S(1)}, f32[8,128]{1,0:T(8,128)S(1)}, u32[]{:S(2)}, u32[]{:S(2)}) collective-permute-start(f32[8,128]{1,0:T(8,128)S(1)} %add.64), channel_id=1, source_target_pairs={{0,8},{4,12},{8,0},{12,4},{16,24},{20,28},{24,16},{28,20},{1,9},{5... | collective-permute-start | bytes 12296 | tf_op jit(solution)/shard_map/ppermute | solution.py:428
  68.3 0.7 collective-permute-start.24
  69.0 1.0 collective-permute-done.26
  70.0 1.9 %collective-permute-done.24 = f32[8,128]{1,0:T(8,128)S(1)} collective-permute-done((f32[8,128]{1,0:T(8,128)S(1)}, f32[8,128]{1,0:T(8,128)S(1)}, u32[]{:S(2)}, u32[]{:S(2)}) %collective-permute-start.24) | collective-permute-done | bytes 4128 | tf_op jit(solution)/shard_map/ppermute | solution.py:428
  72.0 2.9 %shard_map.119 = (f32[512,128]{1,0:T(8,128)S(1)}, f32[256,128]{1,0:T(8,128)S(1)}, f32[256,128]{1,0:T(8,128)S(1)}) custom-call(s32[512]{0:T(512)S(1)} %pad_add_fusion.ids_ref, bf16[256,128,128]{2,1,0:T(8,128)(2,1)S(1)} %get-tuple-element.59.turned, f32[256,128]{1,0:T(8,128)S(1)} %add_select_fusion.refs_0_, f32[256,128]{1,0:T(8,128)S(1)} %collective-permute-done.14.refs_1_, ...), custom_call_target="tpu_custom_call" | custom-call | flops 8388608 | bytes 8388608 | tf_op jit(solution)/shard_map/pallas_call | solution.py:410
  75.0 1.3 %collective-permute-done.27 = f32[256,128]{1,0:T(8,128)S(1)} collective-permute-done((f32[256,128]{1,0:T(8,128)S(1)}, f32[256,128]{1,0:T(8,128)S(1)}, u32[]{:S(2)}, u32[]{:S(2)}) %collective-permute-start.27) | collective-permute-done | bytes 131104 | tf_op jit(solution)/shard_map/ppermute | solution.py:428
  76.4 1.5 %collective-permute-start.28 = (f32[256,128]{1,0:T(8,128)S(1)}, f32[256,128]{1,0:T(8,128)S(1)}, u32[]{:S(2)}, u32[]{:S(2)}) collective-permute-start(f32[256,128]{1,0:T(8,128)S(1)} %add.68), channel_id=1, source_target_pairs={{0,2},{1,3},{2,0},{3,1},{4,6},{5,7},{6,4},{7,5},{8,10},{9,11},{10,... | collective-permute-start | bytes 393224 | tf_op jit(solution)/shard_map/ppermute | solution.py:428
  77.9 4.1 %collective-permute-done.28 = f32[256,128]{1,0:T(8,128)S(1)} collective-permute-done((f32[256,128]{1,0:T(8,128)S(1)}, f32[256,128]{1,0:T(8,128)S(1)}, u32[]{:S(2)}, u32[]{:S(2)}) %collective-permute-start.28) | collective-permute-done | bytes 131104 | tf_op jit(solution)/shard_map/ppermute | solution.py:428
  82.1 1.3 %collective-permute-done.29.refs_1_ = f32[256,128]{1,0:T(8,128)S(1)} collective-permute-done((f32[256,128]{1,0:T(8,128)S(1)}, f32[256,128]{1,0:T(8,128)S(1)}, u32[]{:S(2)}, u32[]{:S(2)}) %collective-permute-start.29) | collective-permute-done | bytes 131104 | tf_op jit(solution)/shard_map/ppermute | solution.py:428
  83.4 2.8 %shard_map.120 = (f32[512,128]{1,0:T(8,128)S(1)}, f32[128,128]{1,0:T(8,128)S(1)}, f32[128,128]{1,0:T(8,128)S(1)}, f32[128,128]{1,0:T(8,128)S(1)}, f32[128,128]{1,0:T(8,128)S(1)}) custom-call(s32[512]{0:T(512)S(1)} %pad_add_fusion.ids_ref, bf16[256,128,128]{2,1,0:T(8,128)(2,1)S(1)} %get-tuple-element.49.blocks, f32[256,128]{1,0:T(8,128)S(1)} %add.69.refs_0_, ...), custom_call_target="tpu_custom_call" | custom-call | flops 8388608 | bytes 8388608 | tf_op jit(solution)/shard_map/pallas_call | solution.py:410
  86.2 0.5 collective-permute-start.30
  86.7 0.5 collective-permute-start.31
  87.2 2.6 %collective-permute-start.32 = (f32[128,128]{1,0:T(8,128)S(1)}, f32[128,128]{1,0:T(8,128)S(1)}, u32[]{:S(2)}, u32[]{:S(2)}) collective-permute-start(f32[128,128]{1,0:T(8,128)S(1)} %get-tuple-element.90), channel_id=1, source_target_pairs={{0,12},{4,8},{8,4},{12,0},{16,28},{20,24},{24,20},{28,16},{1,13},{... | collective-permute-start | bytes 196616 | tf_op jit(solution)/shard_map/ppermute | solution.py:428
  89.8 0.8 collective-permute-done.30
  90.6 1.1 collective-permute-done.31
  91.6 1.4 %collective-permute-done.32 = f32[128,128]{1,0:T(8,128)S(1)} collective-permute-done((f32[128,128]{1,0:T(8,128)S(1)}, f32[128,128]{1,0:T(8,128)S(1)}, u32[]{:S(2)}, u32[]{:S(2)}) %collective-permute-start.32) | collective-permute-done | bytes 65568 | tf_op jit(solution)/shard_map/ppermute | solution.py:428
  93.0 0.7 collective-permute-start.33
  93.8 5.2 %collective-permute-done.33 = f32[128,128]{1,0:T(8,128)S(1)} collective-permute-done((f32[128,128]{1,0:T(8,128)S(1)}, f32[128,128]{1,0:T(8,128)S(1)}, u32[]{:S(2)}, u32[]{:S(2)}) %collective-permute-start.33) | collective-permute-done | bytes 65568 | tf_op jit(solution)/shard_map/ppermute | solution.py:428
  99.0 1.6 %collective-permute-start.36 = (f32[128,128]{1,0:T(8,128)S(1)}, f32[128,128]{1,0:T(8,128)S(1)}, u32[]{:S(2)}, u32[]{:S(2)}) collective-permute-start(f32[128,128]{1,0:T(8,128)S(1)} %add.73.refs_0_), channel_id=1, source_target_pairs={{0,12},{4,8},{8,4},{12,0},{16,28},{20,24},{24,20},{28,16},{1,13},{... | collective-permute-start | bytes 196616 | tf_op jit(solution)/shard_map/ppermute | solution.py:428
  100.6 1.9 %collective-permute-start.34 = (f32[128,128]{1,0:T(8,128)S(1)}, f32[128,128]{1,0:T(8,128)S(1)}, u32[]{:S(2)}, u32[]{:S(2)}) collective-permute-start(f32[128,128]{1,0:T(8,128)S(1)} %add.73.refs_0_), channel_id=1, source_target_pairs={{0,4},{4,0},{8,12},{12,8},{16,20},{20,16},{24,28},{28,24},{1,5},{5... | collective-permute-start | bytes 196616 | tf_op jit(solution)/shard_map/ppermute | solution.py:428
  102.5 1.7 %collective-permute-done.36.refs_3_ = f32[128,128]{1,0:T(8,128)S(1)} collective-permute-done((f32[128,128]{1,0:T(8,128)S(1)}, f32[128,128]{1,0:T(8,128)S(1)}, u32[]{:S(2)}, u32[]{:S(2)}) %collective-permute-start.36) | collective-permute-done | bytes 65568 | tf_op jit(solution)/shard_map/ppermute | solution.py:428
  104.2 0.7 collective-permute-done.35.refs_2_
  104.9 3.0 %shard_map.121 = (f32[512,128]{1,0:T(8,128)}, f32[256,128]{1,0:T(8,128)S(1)}, f32[256,128]{1,0:T(8,128)S(1)}) custom-call(s32[512]{0:T(512)S(1)} %pad_add_fusion.ids_ref, bf16[256,128,128]{2,1,0:T(8,128)(2,1)S(1)} %get-tuple-element.59.turned, f32[128,128]{1,0:T(8,128)S(1)} %add.73.refs_0_, f32[128,128]{1,0:T(8,128)S(1)} %collective-permute-done.34.refs_1_, ...), custom_call_target="tpu_custom_call" | custom-call | flops 8388608 | bytes 8388608 | tf_op jit(solution)/shard_map/pallas_call | solution.py:410
  108.0 1.3 %collective-permute-done.37 = f32[256,128]{1,0:T(8,128)S(1)} collective-permute-done((f32[256,128]{1,0:T(8,128)S(1)}, f32[256,128]{1,0:T(8,128)S(1)}, u32[]{:S(2)}, u32[]{:S(2)}) %collective-permute-start.37) | collective-permute-done | bytes 131104 | tf_op jit(solution)/shard_map/ppermute | solution.py:428
  109.3 1.3 %collective-permute-start.38 = (f32[256,128]{1,0:T(8,128)S(1)}, f32[256,128]{1,0:T(8,128)S(1)}, u32[]{:S(2)}, u32[]{:S(2)}) collective-permute-start(f32[256,128]{1,0:T(8,128)S(1)} %add.74), channel_id=1, source_target_pairs={{0,2},{1,3},{2,0},{3,1},{4,6},{5,7},{6,4},{7,5},{8,10},{9,11},{10,... | collective-permute-start | bytes 393224 | tf_op jit(solution)/shard_map/ppermute | solution.py:428
  110.6 4.3 %collective-permute-done.38 = f32[256,128]{1,0:T(8,128)S(1)} collective-permute-done((f32[256,128]{1,0:T(8,128)S(1)}, f32[256,128]{1,0:T(8,128)S(1)}, u32[]{:S(2)}, u32[]{:S(2)}) %collective-permute-start.38) | collective-permute-done | bytes 131104 | tf_op jit(solution)/shard_map/ppermute | solution.py:428
  115.0 1.3 %collective-permute-done.39.refs_1_ = f32[256,128]{1,0:T(8,128)S(1)} collective-permute-done((f32[256,128]{1,0:T(8,128)S(1)}, f32[256,128]{1,0:T(8,128)S(1)}, u32[]{:S(2)}, u32[]{:S(2)}) %collective-permute-start.39) | collective-permute-done | bytes 131104 | tf_op jit(solution)/shard_map/ppermute | solution.py:428
  116.4 0.9 shard_map.122
  (59 shorter events, 1.3 us)
Async XLA Ops:
  0.6 20.8 %copy-start.2 = (f32[65536]{0:T(1024)S(1)}, f32[65536]{0:T(1024)}, u32[]{:S(2)}) copy-start(f32[65536]{0:T(1024)} %param.19) | copy-start | bytes 786436
  7.1 1.5 %collective-permute-start = (f32[256,128]{1,0:T(8,128)S(1)}, f32[256,128]{1,0:T(8,128)S(1)}, u32[]{:S(2)}, u32[]{:S(2)}) collective-permute-start(f32[256,128]{1,0:T(8,128)S(1)} %get-tuple-element.54), channel_id=1, source_target_pairs={{0,1},{1,0},{2,3},{3,2},{4,5},{5,4},{6,7},{7,6},{8,9},{9,8},{10,11... | collective-permute-start | bytes 393224 | tf_op jit(solution)/shard_map/ppermute | solution.py:428
  8.6 6.7 %collective-permute-start.4 = (f32[256,128]{1,0:T(8,128)S(1)}, f32[256,128]{1,0:T(8,128)S(1)}, u32[]{:S(2)}, u32[]{:S(2)}) collective-permute-start(f32[256,128]{1,0:T(8,128)S(1)} %max.36), channel_id=1, source_target_pairs={{0,2},{1,3},{2,0},{3,1},{4,6},{5,7},{6,4},{7,5},{8,10},{9,11},{10,... | collective-permute-start | bytes 393224 | tf_op jit(solution)/shard_map/ppermute | solution.py:428
  11.5 5.2 %collective-permute-start.3 = (f32[128,128]{1,0:T(8,128)S(1)}, f32[128,128]{1,0:T(8,128)S(1)}, u32[]{:S(2)}, u32[]{:S(2)}) collective-permute-start(f32[128,128]{1,0:T(8,128)S(1)} %get-tuple-element.57), channel_id=1, source_target_pairs={{0,12},{4,8},{8,4},{12,0},{16,28},{20,24},{24,20},{28,16},{1,13},{... | collective-permute-start | bytes 196616 | tf_op jit(solution)/shard_map/ppermute | solution.py:428
  14.0 4.3 %collective-permute-start.1 = (f32[128,128]{1,0:T(8,128)S(1)}, f32[128,128]{1,0:T(8,128)S(1)}, u32[]{:S(2)}, u32[]{:S(2)}) collective-permute-start(f32[128,128]{1,0:T(8,128)S(1)} %get-tuple-element.55), channel_id=1, source_target_pairs={{0,4},{4,0},{8,12},{12,8},{16,20},{20,16},{24,28},{28,24},{1,5},{5... | collective-permute-start | bytes 196616 | tf_op jit(solution)/shard_map/ppermute | solution.py:428
  14.6 4.3 %collective-permute-start.2 = (f32[128,128]{1,0:T(8,128)S(1)}, f32[128,128]{1,0:T(8,128)S(1)}, u32[]{:S(2)}, u32[]{:S(2)}) collective-permute-start(f32[128,128]{1,0:T(8,128)S(1)} %get-tuple-element.56), channel_id=1, source_target_pairs={{0,8},{4,12},{8,0},{12,4},{16,24},{20,28},{24,16},{28,20},{1,9},{5... | collective-permute-start | bytes 196616 | tf_op jit(solution)/shard_map/ppermute | solution.py:428
  15.3 12.9 %collective-permute-start.5 = (f32[256,128]{1,0:T(8,128)S(1)}, f32[256,128]{1,0:T(8,128)S(1)}, u32[]{:S(2)}, u32[]{:S(2)}) collective-permute-start(f32[256,128]{1,0:T(8,128)S(1)} %max.40.refs_0_), channel_id=1, source_target_pairs={{0,1},{1,0},{2,3},{3,2},{4,5},{5,4},{6,7},{7,6},{8,9},{9,8},{10,11... | collective-permute-start | bytes 393224 | tf_op jit(solution)/shard_map/ppermute | solution.py:428
  18.8 5.8 %collective-permute-start.6 = (f32[128,128]{1,0:T(8,128)S(1)}, f32[128,128]{1,0:T(8,128)S(1)}, u32[]{:S(2)}, u32[]{:S(2)}) collective-permute-start(f32[128,128]{1,0:T(8,128)S(1)} %maximum_maximum_fusion), channel_id=1, source_target_pairs={{0,16},{4,20},{8,24},{12,28},{16,0},{20,4},{24,8},{28,12},{1,17},{... | collective-permute-start | bytes 196616 | tf_op jit(solution)/shard_map/ppermute | solution.py:428
  24.7 33.1 %copy-start = (f32[65536]{0:T(1024)S(1)}, f32[65536]{0:T(1024)}, u32[]{:S(2)}) copy-start(f32[65536]{0:T(1024)} %param.14) | copy-start | bytes 786436
  24.7 38.8 %copy-start.1 = (f32[65536]{0:T(1024)S(1)}, f32[65536]{0:T(1024)}, u32[]{:S(2)}) copy-start(f32[65536]{0:T(1024)} %param.13) | copy-start | bytes 786436
  24.7 9.4 %collective-permute-start.9 = (f32[128,128]{1,0:T(8,128)S(1)}, f32[128,128]{1,0:T(8,128)S(1)}, u32[]{:S(2)}, u32[]{:S(2)}) collective-permute-start(f32[128,128]{1,0:T(8,128)S(1)} %max.41.refs_0_), channel_id=1, source_target_pairs={{0,12},{4,8},{8,4},{12,0},{16,28},{20,24},{24,20},{28,16},{1,13},{... | collective-permute-start | bytes 196616 | tf_op jit(solution)/shard_map/ppermute | solution.py:428
  26.3 7.8 %collective-permute-start.8 = (f32[128,128]{1,0:T(8,128)S(1)}, f32[128,128]{1,0:T(8,128)S(1)}, u32[]{:S(2)}, u32[]{:S(2)}) collective-permute-start(f32[128,128]{1,0:T(8,128)S(1)} %max.41.refs_0_), channel_id=1, source_target_pairs={{0,8},{4,12},{8,0},{12,4},{16,24},{20,28},{24,16},{28,20},{1,9},{5... | collective-permute-start | bytes 196616 | tf_op jit(solution)/shard_map/ppermute | solution.py:428
  27.8 6.3 %collective-permute-start.7 = (f32[128,128]{1,0:T(8,128)S(1)}, f32[128,128]{1,0:T(8,128)S(1)}, u32[]{:S(2)}, u32[]{:S(2)}) collective-permute-start(f32[128,128]{1,0:T(8,128)S(1)} %max.41.refs_0_), channel_id=1, source_target_pairs={{0,4},{4,0},{8,12},{12,8},{16,20},{20,16},{24,28},{28,24},{1,5},{5... | collective-permute-start | bytes 196616 | tf_op jit(solution)/shard_map/ppermute | solution.py:428
  34.0 37.9 %copy-start.3 = (f32[65536]{0:T(1024)S(1)}, f32[65536]{0:T(1024)}, u32[]{:S(2)}) copy-start(f32[65536]{0:T(1024)} %param.15) | copy-start | bytes 786436
  34.0 37.9 %copy-start.4 = (f32[65536]{0:T(1024)S(1)}, f32[65536]{0:T(1024)}, u32[]{:S(2)}) copy-start(f32[65536]{0:T(1024)} %param.16) | copy-start | bytes 786436
  34.0 37.9 %copy-start.5 = (s32[65536]{0:T(1024)S(1)}, s32[65536]{0:T(1024)}, u32[]{:S(2)}) copy-start(s32[65536]{0:T(1024)} %param.17) | copy-start | bytes 786436
  34.1 37.9 %copy-start.6 = (f32[65536]{0:T(1024)S(1)}, f32[65536]{0:T(1024)}, u32[]{:S(2)}) copy-start(f32[65536]{0:T(1024)} %param.18) | copy-start | bytes 786436
  34.1 9.0 %collective-permute-start.10 = (f32[256,128]{1,0:T(8,128)S(1)}, f32[256,128]{1,0:T(8,128)S(1)}, u32[]{:S(2)}, u32[]{:S(2)}) collective-permute-start(f32[256,128]{1,0:T(8,128)S(1)} %get-tuple-element.72), channel_id=1, source_target_pairs={{0,4},{4,0},{8,12},{12,8},{16,20},{20,16},{24,28},{28,24},{1,5},{5... | collective-permute-start | bytes 393224 | tf_op jit(solution)/shard_map/ppermute | solution.py:428
  35.7 7.4 %collective-permute-start.11 = (f32[256,128]{1,0:T(8,128)S(1)}, f32[256,128]{1,0:T(8,128)S(1)}, u32[]{:S(2)}, u32[]{:S(2)}) collective-permute-start(f32[256,128]{1,0:T(8,128)S(1)} %get-tuple-element.73), channel_id=1, source_target_pairs={{0,8},{4,12},{8,0},{12,4},{16,24},{20,28},{24,16},{28,20},{1,9},{5... | collective-permute-start | bytes 393224 | tf_op jit(solution)/shard_map/ppermute | solution.py:428
  36.2 6.8 %collective-permute-start.12 = (f32[256,128]{1,0:T(8,128)S(1)}, f32[256,128]{1,0:T(8,128)S(1)}, u32[]{:S(2)}, u32[]{:S(2)}) collective-permute-start(f32[256,128]{1,0:T(8,128)S(1)} %get-tuple-element.74), channel_id=1, source_target_pairs={{0,12},{4,8},{8,4},{12,0},{16,28},{20,24},{24,20},{28,16},{1,13},{... | collective-permute-start | bytes 393224 | tf_op jit(solution)/shard_map/ppermute | solution.py:428
  43.2 1.4 %collective-permute-start.20 = (f32[256,128]{1,0:T(8,128)S(1)}, f32[256,128]{1,0:T(8,128)S(1)}, u32[]{:S(2)}, u32[]{:S(2)}) collective-permute-start(f32[256,128]{1,0:T(8,128)S(1)} %get-tuple-element.81), channel_id=1, source_target_pairs={{0,1},{1,0},{2,3},{3,2},{4,5},{5,4},{6,7},{7,6},{8,9},{9,8},{10,11... | collective-permute-start | bytes 393224 | tf_op jit(solution)/shard_map/ppermute | solution.py:428
  44.6 5.6 %collective-permute-start.21 = (f32[256,128]{1,0:T(8,128)S(1)}, f32[256,128]{1,0:T(8,128)S(1)}, u32[]{:S(2)}, u32[]{:S(2)}) collective-permute-start(f32[256,128]{1,0:T(8,128)S(1)} %max.46), channel_id=1, source_target_pairs={{0,2},{1,3},{2,0},{3,1},{4,6},{5,7},{6,4},{7,5},{8,10},{9,11},{10,... | collective-permute-start | bytes 393224 | tf_op jit(solution)/shard_map/ppermute | solution.py:428
  45.2 8.9 %collective-permute-start.13 = (f32[256,128]{1,0:T(8,128)S(1)}, f32[256,128]{1,0:T(8,128)S(1)}, u32[]{:S(2)}, u32[]{:S(2)}) collective-permute-start(f32[256,128]{1,0:T(8,128)S(1)} %add_select_fusion.1), channel_id=1, source_target_pairs={{0,16},{4,20},{8,24},{12,28},{16,0},{20,4},{24,8},{28,12},{1,17},{... | collective-permute-start | bytes 393224 | tf_op jit(solution)/shard_map/ppermute | solution.py:428
  50.3 7.5 %collective-permute-start.22 = (f32[256,128]{1,0:T(8,128)S(1)}, f32[256,128]{1,0:T(8,128)S(1)}, u32[]{:S(2)}, u32[]{:S(2)}) collective-permute-start(f32[256,128]{1,0:T(8,128)S(1)} %max.47.near), channel_id=1, source_target_pairs={{0,1},{1,0},{2,3},{3,2},{4,5},{5,4},{6,7},{7,6},{8,9},{9,8},{10,11... | collective-permute-start | bytes 393224 | tf_op jit(solution)/shard_map/ppermute | solution.py:428
  54.2 7.3 %collective-permute-start.16 = (f32[256,128]{1,0:T(8,128)S(1)}, f32[256,128]{1,0:T(8,128)S(1)}, u32[]{:S(2)}, u32[]{:S(2)}) collective-permute-start(f32[256,128]{1,0:T(8,128)S(1)} %add_select_fusion.refs_0_), channel_id=1, source_target_pairs={{0,12},{4,8},{8,4},{12,0},{16,28},{20,24},{24,20},{28,16},{1,13},{... | collective-permute-start | bytes 393224 | tf_op jit(solution)/shard_map/ppermute | solution.py:428
  54.3 9.1 %collective-permute-start.15 = (f32[256,128]{1,0:T(8,128)S(1)}, f32[256,128]{1,0:T(8,128)S(1)}, u32[]{:S(2)}, u32[]{:S(2)}) collective-permute-start(f32[256,128]{1,0:T(8,128)S(1)} %add_select_fusion.refs_0_), channel_id=1, source_target_pairs={{0,8},{4,12},{8,0},{12,4},{16,24},{20,28},{24,16},{28,20},{1,9},{5... | collective-permute-start | bytes 393224 | tf_op jit(solution)/shard_map/ppermute | solution.py:428
  57.2 6.3 %collective-permute-start.14 = (f32[256,128]{1,0:T(8,128)S(1)}, f32[256,128]{1,0:T(8,128)S(1)}, u32[]{:S(2)}, u32[]{:S(2)}) collective-permute-start(f32[256,128]{1,0:T(8,128)S(1)} %add_select_fusion.refs_0_), channel_id=1, source_target_pairs={{0,4},{4,0},{8,12},{12,8},{16,20},{20,16},{24,28},{28,24},{1,5},{5... | collective-permute-start | bytes 393224 | tf_op jit(solution)/shard_map/ppermute | solution.py:428
  57.9 7.6 %collective-permute-start.23 = (f32[8,128]{1,0:T(8,128)S(1)}, f32[8,128]{1,0:T(8,128)S(1)}, u32[]{:S(2)}, u32[]{:S(2)}) collective-permute-start(f32[8,128]{1,0:T(8,128)S(1)} %get-tuple-element.83), channel_id=1, source_target_pairs={{0,16},{4,20},{8,24},{12,28},{16,0},{20,4},{24,8},{28,12},{1,17},{... | collective-permute-start | bytes 12296 | tf_op jit(solution)/shard_map/ppermute | solution.py:428
  63.6 4.8 %collective-permute-start.19 = (f32[8,128]{1,0:T(8,128)S(1)}, f32[8,128]{1,0:T(8,128)S(1)}, u32[]{:S(2)}, u32[]{:S(2)}) collective-permute-start(f32[8,128]{1,0:T(8,128)S(1)} %get-tuple-element.77), channel_id=1, source_target_pairs={{0,3},{1,2},{2,1},{3,0},{4,7},{5,6},{6,5},{7,4},{8,11},{9,10},{10,... | collective-permute-start | bytes 12296 | tf_op jit(solution)/shard_map/ppermute | solution.py:428
  64.1 4.9 %collective-permute-start.18 = (f32[8,128]{1,0:T(8,128)S(1)}, f32[8,128]{1,0:T(8,128)S(1)}, u32[]{:S(2)}, u32[]{:S(2)}) collective-permute-start(f32[8,128]{1,0:T(8,128)S(1)} %get-tuple-element.77), channel_id=1, source_target_pairs={{0,2},{1,3},{2,0},{3,1},{4,6},{5,7},{6,4},{7,5},{8,10},{9,11},{10,... | collective-permute-start | bytes 12296 | tf_op jit(solution)/shard_map/ppermute | solution.py:428
  65.2 3.7 %collective-permute-start.17 = (f32[8,128]{1,0:T(8,128)S(1)}, f32[8,128]{1,0:T(8,128)S(1)}, u32[]{:S(2)}, u32[]{:S(2)}) collective-permute-start(f32[8,128]{1,0:T(8,128)S(1)} %get-tuple-element.77), channel_id=1, source_target_pairs={{0,1},{1,0},{2,3},{3,2},{4,5},{5,4},{6,7},{7,6},{8,9},{9,8},{10,11... | collective-permute-start | bytes 12296 | tf_op jit(solution)/shard_map/ppermute | solution.py:428
  65.5 4.5 %collective-permute-start.26 = (f32[8,128]{1,0:T(8,128)S(1)}, f32[8,128]{1,0:T(8,128)S(1)}, u32[]{:S(2)}, u32[]{:S(2)}) collective-permute-start(f32[8,128]{1,0:T(8,128)S(1)} %add.64), channel_id=1, source_target_pairs={{0,12},{4,8},{8,4},{12,0},{16,28},{20,24},{24,20},{28,16},{1,13},{... | collective-permute-start | bytes 12296 | tf_op jit(solution)/shard_map/ppermute | solution.py:428
  65.7 4.3 %collective-permute-start.25 = (f32[8,128]{1,0:T(8,128)S(1)}, f32[8,128]{1,0:T(8,128)S(1)}, u32[]{:S(2)}, u32[]{:S(2)}) collective-permute-start(f32[8,128]{1,0:T(8,128)S(1)} %add.64), channel_id=1, source_target_pairs={{0,8},{4,12},{8,0},{12,4},{16,24},{20,28},{24,16},{28,20},{1,9},{5... | collective-permute-start | bytes 12296 | tf_op jit(solution)/shard_map/ppermute | solution.py:428
  68.3 3.6 %collective-permute-start.24 = (f32[8,128]{1,0:T(8,128)S(1)}, f32[8,128]{1,0:T(8,128)S(1)}, u32[]{:S(2)}, u32[]{:S(2)}) collective-permute-start(f32[8,128]{1,0:T(8,128)S(1)} %add.64), channel_id=1, source_target_pairs={{0,4},{4,0},{8,12},{12,8},{16,20},{20,16},{24,28},{28,24},{1,5},{5... | collective-permute-start | bytes 12296 | tf_op jit(solution)/shard_map/ppermute | solution.py:428
  74.9 1.4 %collective-permute-start.27 = (f32[256,128]{1,0:T(8,128)S(1)}, f32[256,128]{1,0:T(8,128)S(1)}, u32[]{:S(2)}, u32[]{:S(2)}) collective-permute-start(f32[256,128]{1,0:T(8,128)S(1)} %get-tuple-element.85), channel_id=1, source_target_pairs={{0,1},{1,0},{2,3},{3,2},{4,5},{5,4},{6,7},{7,6},{8,9},{9,8},{10,11... | collective-permute-start | bytes 393224 | tf_op jit(solution)/shard_map/ppermute | solution.py:428
  76.4 5.6 %collective-permute-start.28 = (f32[256,128]{1,0:T(8,128)S(1)}, f32[256,128]{1,0:T(8,128)S(1)}, u32[]{:S(2)}, u32[]{:S(2)}) collective-permute-start(f32[256,128]{1,0:T(8,128)S(1)} %add.68), channel_id=1, source_target_pairs={{0,2},{1,3},{2,0},{3,1},{4,6},{5,7},{6,4},{7,5},{8,10},{9,11},{10,... | collective-permute-start | bytes 393224 | tf_op jit(solution)/shard_map/ppermute | solution.py:428
  82.0 1.4 %collective-permute-start.29 = (f32[256,128]{1,0:T(8,128)S(1)}, f32[256,128]{1,0:T(8,128)S(1)}, u32[]{:S(2)}, u32[]{:S(2)}) collective-permute-start(f32[256,128]{1,0:T(8,128)S(1)} %add.69.refs_0_), channel_id=1, source_target_pairs={{0,1},{1,0},{2,3},{3,2},{4,5},{5,4},{6,7},{7,6},{8,9},{9,8},{10,11... | collective-permute-start | bytes 393224 | tf_op jit(solution)/shard_map/ppermute | solution.py:428
  86.2 4.3 %collective-permute-start.30 = (f32[128,128]{1,0:T(8,128)S(1)}, f32[128,128]{1,0:T(8,128)S(1)}, u32[]{:S(2)}, u32[]{:S(2)}) collective-permute-start(f32[128,128]{1,0:T(8,128)S(1)} %get-tuple-element.88), channel_id=1, source_target_pairs={{0,4},{4,0},{8,12},{12,8},{16,20},{20,16},{24,28},{28,24},{1,5},{5... | collective-permute-start | bytes 196616 | tf_op jit(solution)/shard_map/ppermute | solution.py:428
  86.7 4.9 %collective-permute-start.31 = (f32[128,128]{1,0:T(8,128)S(1)}, f32[128,128]{1,0:T(8,128)S(1)}, u32[]{:S(2)}, u32[]{:S(2)}) collective-permute-start(f32[128,128]{1,0:T(8,128)S(1)} %get-tuple-element.89), channel_id=1, source_target_pairs={{0,8},{4,12},{8,0},{12,4},{16,24},{20,28},{24,16},{28,20},{1,9},{5... | collective-permute-start | bytes 196616 | tf_op jit(solution)/shard_map/ppermute | solution.py:428
  87.2 5.9 %collective-permute-start.32 = (f32[128,128]{1,0:T(8,128)S(1)}, f32[128,128]{1,0:T(8,128)S(1)}, u32[]{:S(2)}, u32[]{:S(2)}) collective-permute-start(f32[128,128]{1,0:T(8,128)S(1)} %get-tuple-element.90), channel_id=1, source_target_pairs={{0,12},{4,8},{8,4},{12,0},{16,28},{20,24},{24,20},{28,16},{1,13},{... | collective-permute-start | bytes 196616 | tf_op jit(solution)/shard_map/ppermute | solution.py:428
  93.0 5.9 %collective-permute-start.33 = (f32[128,128]{1,0:T(8,128)S(1)}, f32[128,128]{1,0:T(8,128)S(1)}, u32[]{:S(2)}, u32[]{:S(2)}) collective-permute-start(f32[128,128]{1,0:T(8,128)S(1)} %add_add_fusion), channel_id=1, source_target_pairs={{0,16},{4,20},{8,24},{12,28},{16,0},{20,4},{24,8},{28,12},{1,17},{... | collective-permute-start | bytes 196616 | tf_op jit(solution)/shard_map/ppermute | solution.py:428
  99.0 5.2 %collective-permute-start.36 = (f32[128,128]{1,0:T(8,128)S(1)}, f32[128,128]{1,0:T(8,128)S(1)}, u32[]{:S(2)}, u32[]{:S(2)}) collective-permute-start(f32[128,128]{1,0:T(8,128)S(1)} %add.73.refs_0_), channel_id=1, source_target_pairs={{0,12},{4,8},{8,4},{12,0},{16,28},{20,24},{24,20},{28,16},{1,13},{... | collective-permute-start | bytes 196616 | tf_op jit(solution)/shard_map/ppermute | solution.py:428
  100.6 4.3 %collective-permute-start.35 = (f32[128,128]{1,0:T(8,128)S(1)}, f32[128,128]{1,0:T(8,128)S(1)}, u32[]{:S(2)}, u32[]{:S(2)}) collective-permute-start(f32[128,128]{1,0:T(8,128)S(1)} %add.73.refs_0_), channel_id=1, source_target_pairs={{0,8},{4,12},{8,0},{12,4},{16,24},{20,28},{24,16},{28,20},{1,9},{5... | collective-permute-start | bytes 196616 | tf_op jit(solution)/shard_map/ppermute | solution.py:428
  100.6 4.3 %collective-permute-start.34 = (f32[128,128]{1,0:T(8,128)S(1)}, f32[128,128]{1,0:T(8,128)S(1)}, u32[]{:S(2)}, u32[]{:S(2)}) collective-permute-start(f32[128,128]{1,0:T(8,128)S(1)} %add.73.refs_0_), channel_id=1, source_target_pairs={{0,4},{4,0},{8,12},{12,8},{16,20},{20,16},{24,28},{28,24},{1,5},{5... | collective-permute-start | bytes 196616 | tf_op jit(solution)/shard_map/ppermute | solution.py:428
  107.9 1.4 %collective-permute-start.37 = (f32[256,128]{1,0:T(8,128)S(1)}, f32[256,128]{1,0:T(8,128)S(1)}, u32[]{:S(2)}, u32[]{:S(2)}) collective-permute-start(f32[256,128]{1,0:T(8,128)S(1)} %get-tuple-element.94), channel_id=1, source_target_pairs={{0,1},{1,0},{2,3},{3,2},{4,5},{5,4},{6,7},{7,6},{8,9},{9,8},{10,11... | collective-permute-start | bytes 393224 | tf_op jit(solution)/shard_map/ppermute | solution.py:428
  109.3 5.6 %collective-permute-start.38 = (f32[256,128]{1,0:T(8,128)S(1)}, f32[256,128]{1,0:T(8,128)S(1)}, u32[]{:S(2)}, u32[]{:S(2)}) collective-permute-start(f32[256,128]{1,0:T(8,128)S(1)} %add.74), channel_id=1, source_target_pairs={{0,2},{1,3},{2,0},{3,1},{4,6},{5,7},{6,4},{7,5},{8,10},{9,11},{10,... | collective-permute-start | bytes 393224 | tf_op jit(solution)/shard_map/ppermute | solution.py:428
  115.0 1.4 %collective-permute-start.39 = (f32[256,128]{1,0:T(8,128)S(1)}, f32[256,128]{1,0:T(8,128)S(1)}, u32[]{:S(2)}, u32[]{:S(2)}) collective-permute-start(f32[256,128]{1,0:T(8,128)S(1)} %add.75.refs_0_), channel_id=1, source_target_pairs={{0,1},{1,0},{2,3},{3,2},{4,5},{5,4},{6,7},{7,6},{8,9},{9,8},{10,11... | collective-permute-start | bytes 393224 | tf_op jit(solution)/shard_map/ppermute | solution.py:428
